TPU v7x, 512 devices: a whole 4x4x16 slice. The times are simulated.
512 devices in a mesh: row: 32 (over z, core), col: 16 (over y, x).
Axes of the slice: x: 4, y: 4, z: 16, core: 2. Of those that a mesh axis runs over, the one named last changes fastest.
Arguments:
- a_blocks: bfloat16 [32, 16, 96, 128, 128], P('row', 'col'), may hold values from -0.5 to 0.5
- a_rows: int32 [32, 16, 96], P('row', 'col'), may hold values from 0 to 31, as said below
- a_cols: int32 [32, 16, 96], P('row', 'col'), may hold values from 0 to 63, as said below
- p_blocks: bfloat16 [1024, 128, 256], P(('row', 'col')), may hold values from -0.5 to 0.5
- coarse_slot: int32 [32, 16, 96, 4, 4], P('row', 'col'), may hold values from 0 to 127
Outputs:
- coarse_blocks: bfloat16 [32, 128, 4096], P('row', 'col')
Inputs may be any that keep to these rules, and one draw needn't show every extreme that they name: On each owner the pairs (a_rows, a_cols) of its 96 blocks are distinct. On each owner the pairs (a_rows, a_cols) of its 96 blocks are distinct.
All inputs are finite; a program needn't handle non-finite values.
Results may differ from a plain program's by a relative error of at most 0.0049.
Values may be sent and summed in bfloat16 or wider, within the bound.
A program may use at most 128 MiB of HBM per device.

v0:
```python
import jax
import jax.numpy as jnp
from jax import lax
from jax.sharding import PartitionSpec as P

KS_DEV = 8


def copy_for_each(array, axis):
    size = lax.axis_size(axis)
    return lax.all_to_all(
        jnp.broadcast_to(array[None], (size, *array.shape)), axis, 0, 0, tiled=True
    )


def joined_along(tiles, dim):
    lengths = list(tiles.shape[1:])
    lengths[dim] *= tiles.shape[0]
    return jnp.moveaxis(tiles, 0, dim).reshape(lengths)


def collect(array, axis, dim):
    tiles = copy_for_each(array, axis)
    return joined_along(tiles, dim)


def in_blocks(array, dim, size):
    lengths = array.shape
    tiles = array.reshape(*lengths[:dim], size, lengths[dim] // size, *lengths[dim + 1 :])
    return jnp.moveaxis(tiles, dim, 0)


def sum_at_owner(array, axis, dim):
    tiles = in_blocks(array, dim, lax.axis_size(axis))
    arrived = lax.all_to_all(tiles, axis, split_axis=0, concat_axis=0, tiled=True)
    return arrived.sum(axis=0)


def owner_terms(blocks, row_ids, col_ids, slot_ids, row_panel, column_panel, slot_count):
    count = blocks.shape[0]
    group_size = 16
    groups = count // group_size
    node_width = blocks.shape[1]
    panel_width = row_panel.shape[2]
    agg_blocks = slot_ids.shape[1]
    agg_width = panel_width // agg_blocks

    def accumulate(running, batch_item):
        blk, rws, cls, sls = batch_item
        right_rows = jnp.take(column_panel, cls, axis=0)
        product = jnp.einsum(
            "kab,kbw->kaw", blk, right_rows, preferred_element_type=jnp.float32
        ).astype(jnp.bfloat16)
        left_rows = jnp.take(row_panel, rws, axis=0)
        left_split = left_rows.reshape(group_size, node_width, agg_blocks, agg_width)
        right_split = product.reshape(group_size, node_width, agg_blocks, agg_width)
        contribs = jnp.einsum(
            "knta,knsb->ktsab", left_split, right_split, preferred_element_type=jnp.float32
        )
        contribs = contribs.reshape(group_size * agg_blocks * agg_blocks, agg_width * agg_width)
        running = running.at[sls.reshape(-1)].add(contribs)
        return (running, None)

    items = (
        blocks.reshape(groups, group_size, node_width, node_width),
        row_ids.reshape(groups, group_size),
        col_ids.reshape(groups, group_size),
        slot_ids.reshape(groups, group_size, agg_blocks, agg_blocks),
    )
    start = jnp.zeros((slot_count, agg_width * agg_width), jnp.float32)
    running, _ = lax.scan(accumulate, start, items)
    return running


def on_device(a_blocks, a_rows, a_cols, p_blocks, coarse_slot):
    rows_total = lax.axis_size("row")
    cols_total = lax.axis_size("col")
    fan_count = rows_total // cols_total
    piece_rows = p_blocks.shape[0]
    tail_shape = p_blocks.shape[1:]
    row_panel = collect(p_blocks, "col", 0)
    column_rows = lax.all_gather(p_blocks, "row", axis=0, tiled=True)
    grouped = column_rows.reshape((cols_total, fan_count, piece_rows) + tail_shape)
    regrouped = lax.all_to_all(grouped, "col", split_axis=0, concat_axis=2, tiled=True)
    column_panel = regrouped.reshape((fan_count * cols_total * piece_rows,) + tail_shape)
    slot_count = KS_DEV * cols_total
    running = owner_terms(
        a_blocks[0, 0],
        a_rows[0, 0],
        a_cols[0, 0],
        coarse_slot[0, 0],
        row_panel,
        column_panel,
        slot_count,
    )
    reduced = sum_at_owner(running, "col", 0)
    return reduced.astype(jnp.bfloat16)[None]


def solution(mesh):
    placed = (
        P("row", "col", None, None, None),
        P("row", "col", None),
        P("row", "col", None),
        P(("row", "col"), None, None),
        P("row", "col", None, None, None),
    )
    return jax.shard_map(
        on_device, mesh=mesh, in_specs=placed, out_specs=P("row", "col", None), check_vma=False
    )
```

profile of v0, /device:TPU:1, one launch (start us, length us, event | category | flops | bytes accessed | tf_op | source)
XLA Modules:
  0.0 480.6 jit_solution(17363315479896694393)
XLA Ops:
  7.3 81.7 %all-gather.2.cloned.1.call-done = bf16[64,128,256]{2,1,0:T(8,128)(2,1)} async-done(((bf16[2,128,256]{2,1,0:T(8,128)(2,1)}), bf16[64,128,256]{2,1,0:T(8,128)(2,1)}) %all-gather.2.cloned.1.call-update) | async-done | bytes 4194320 | tf_op jit(solution)/shard_map/all_gather | solution.py:82
  89.0 57.2 %all_to_all.25 = bf16[16,2,2,128,256]{4,3,2,1,0:T(8,128)(2,1)} all-to-all(bf16[16,2,2,128,256]{4,3,2,1,0:T(8,128)(2,1)} %bitcast.70), channel_id=1, replica_groups=mesh['row'=32,'col'=16] {'col'}, dimensions={0} | all-to-all | bytes 8388608 | tf_op jit(solution)/shard_map/all_to_all | solution.py:84
  147.8 3.7 all-to-all-start.1
  153.7 4.6 copy.25
  158.3 21.4 %all-to-all-done.1 = bf16[16,2,128,256]{3,2,1,0:T(8,128)(2,1)S(1)} async-done(((bf16[16,2,128,256]{3,2,1,0:T(8,128)(2,1)}), bf16[16,2,128,256]{3,2,1,0:T(8,128)(2,1)S(1)}, u32[]{:S(2)}, u32[]{:S(2)}) %all-to-all-start.1) | async-done | bytes 2097184 | tf_op jit(solution)/shard_map/all_to_all | solution.py:11
  181.3 257.3 %while.10 = (s32[]{:T(128)}, f32[128,4096]{1,0:T(8,128)S(1)}, s32[6,16,4,4]{3,2,1,0:T(4,128)S(1)}, bf16[6,16,128,128]{3,2,1,0:T(8,128)(2,1)}, s32[6,16]{1,0:T(8,...) while((s32[]{:T(128)}, f32[128,4096]{1,0:T(8,128)S(1)}, ...), condition=%wide.region_2.3_spmd, body=%wide.region_0.2_spmd.sunk | while | flops 405277728 | bytes 46678312 | solution.py:71
  181.3 2.8 gather_fusion
  192.5 6.1 %convolution_bitcast_fusion.2 = f32[16,4,4,64,64]{3,4,1,2,0:T(8,128)} fusion(bf16[16,128,4,64,1]{1,3,4,2,0:T(8,128)(2,1)} %bitcast.66, bf16[16,128,4,64]{1,3,2,0:T(8,128)(2,1)} %bitcast.67, pred[16]{0:T(512)(128)(4,1)S(1)} %get-tuple-element.156), kind=kOutput, calls=%fused_computation.3.clone.1 | convolution fusion | flops 268959744 | bytes 6291472 | tf_op jit(solution)/shard_map/while/body/eval_jaxpr/knta,knsb->ktsab/dot_general | solution.py:57
  198.6 9.3 %copy.35 = f32[16,4,4,64,64]{4,3,2,1,0:T(8,128)} copy(f32[16,4,4,64,64]{3,4,1,2,0:T(8,128)} %convolution_bitcast_fusion.2) | data formatting | bytes 8388608 | tf_op jit(solution)/shard_map/while/body/eval_jaxpr/knta,knsb->ktsab/transpose | solution.py:57
  207.8 7.9 %reshape.191 = f32[256,4096]{1,0:T(8,128)} reshape(f32[16,4,4,64,64]{4,3,2,1,0:T(8,128)} %copy.35) | data formatting | bytes 8388608 | tf_op jit(solution)/shard_map/while/body/eval_jaxpr/reshape | solution.py:60
  215.9 8.3 %scatter_fusion = f32[128,4096]{1,0:T(8,128)S(1)} fusion(f32[128,4096]{1,0:T(8,128)S(1)} %get-tuple-element.167, s32[256]{0:T(256)S(1)} %bitcast.73, f32[256,4096]{1,0:T(8,128)} %reshape.191), kind=kCustom, calls=%fused_computation.2.clone.1 | custom fusion | flops 1048576 | bytes 12583936 | tf_op jit(solution)/shard_map/while/body/eval_jaxpr/scatter-add | solution.py:61
  235.4 6.1 %convolution_bitcast_fusion.2 = f32[16,4,4,64,64]{3,4,1,2,0:T(8,128)} fusion(bf16[16,128,4,64,1]{1,3,4,2,0:T(8,128)(2,1)} %bitcast.66, bf16[16,128,4,64]{1,3,2,0:T(8,128)(2,1)} %bitcast.67, pred[16]{0:T(512)(128)(4,1)S(1)} %get-tuple-element.156), kind=kOutput, calls=%fused_computation.3.clone.1 | convolution fusion | flops 268959744 | bytes 6291472 | tf_op jit(solution)/shard_map/while/body/eval_jaxpr/knta,knsb->ktsab/dot_general | solution.py:57
  241.5 9.3 %copy.35 = f32[16,4,4,64,64]{4,3,2,1,0:T(8,128)} copy(f32[16,4,4,64,64]{3,4,1,2,0:T(8,128)} %convolution_bitcast_fusion.2) | data formatting | bytes 8388608 | tf_op jit(solution)/shard_map/while/body/eval_jaxpr/knta,knsb->ktsab/transpose | solution.py:57
  250.7 7.9 %reshape.191 = f32[256,4096]{1,0:T(8,128)} reshape(f32[16,4,4,64,64]{4,3,2,1,0:T(8,128)} %copy.35) | data formatting | bytes 8388608 | tf_op jit(solution)/shard_map/while/body/eval_jaxpr/reshape | solution.py:60
  258.8 8.3 %scatter_fusion = f32[128,4096]{1,0:T(8,128)S(1)} fusion(f32[128,4096]{1,0:T(8,128)S(1)} %get-tuple-element.167, s32[256]{0:T(256)S(1)} %bitcast.73, f32[256,4096]{1,0:T(8,128)} %reshape.191), kind=kCustom, calls=%fused_computation.2.clone.1 | custom fusion | flops 1048576 | bytes 12583936 | tf_op jit(solution)/shard_map/while/body/eval_jaxpr/scatter-add | solution.py:61
  278.3 6.1 %convolution_bitcast_fusion.2 = f32[16,4,4,64,64]{3,4,1,2,0:T(8,128)} fusion(bf16[16,128,4,64,1]{1,3,4,2,0:T(8,128)(2,1)} %bitcast.66, bf16[16,128,4,64]{1,3,2,0:T(8,128)(2,1)} %bitcast.67, pred[16]{0:T(512)(128)(4,1)S(1)} %get-tuple-element.156), kind=kOutput, calls=%fused_computation.3.clone.1 | convolution fusion | flops 268959744 | bytes 6291472 | tf_op jit(solution)/shard_map/while/body/eval_jaxpr/knta,knsb->ktsab/dot_general | solution.py:57
  284.4 9.3 %copy.35 = f32[16,4,4,64,64]{4,3,2,1,0:T(8,128)} copy(f32[16,4,4,64,64]{3,4,1,2,0:T(8,128)} %convolution_bitcast_fusion.2) | data formatting | bytes 8388608 | tf_op jit(solution)/shard_map/while/body/eval_jaxpr/knta,knsb->ktsab/transpose | solution.py:57
  293.6 7.9 %reshape.191 = f32[256,4096]{1,0:T(8,128)} reshape(f32[16,4,4,64,64]{4,3,2,1,0:T(8,128)} %copy.35) | data formatting | bytes 8388608 | tf_op jit(solution)/shard_map/while/body/eval_jaxpr/reshape | solution.py:60
  301.6 8.3 %scatter_fusion = f32[128,4096]{1,0:T(8,128)S(1)} fusion(f32[128,4096]{1,0:T(8,128)S(1)} %get-tuple-element.167, s32[256]{0:T(256)S(1)} %bitcast.73, f32[256,4096]{1,0:T(8,128)} %reshape.191), kind=kCustom, calls=%fused_computation.2.clone.1 | custom fusion | flops 1048576 | bytes 12583936 | tf_op jit(solution)/shard_map/while/body/eval_jaxpr/scatter-add | solution.py:61
  321.2 6.1 %convolution_bitcast_fusion.2 = f32[16,4,4,64,64]{3,4,1,2,0:T(8,128)} fusion(bf16[16,128,4,64,1]{1,3,4,2,0:T(8,128)(2,1)} %bitcast.66, bf16[16,128,4,64]{1,3,2,0:T(8,128)(2,1)} %bitcast.67, pred[16]{0:T(512)(128)(4,1)S(1)} %get-tuple-element.156), kind=kOutput, calls=%fused_computation.3.clone.1 | convolution fusion | flops 268959744 | bytes 6291472 | tf_op jit(solution)/shard_map/while/body/eval_jaxpr/knta,knsb->ktsab/dot_general | solution.py:57
  327.3 9.3 %copy.35 = f32[16,4,4,64,64]{4,3,2,1,0:T(8,128)} copy(f32[16,4,4,64,64]{3,4,1,2,0:T(8,128)} %convolution_bitcast_fusion.2) | data formatting | bytes 8388608 | tf_op jit(solution)/shard_map/while/body/eval_jaxpr/knta,knsb->ktsab/transpose | solution.py:57
  336.5 7.9 %reshape.191 = f32[256,4096]{1,0:T(8,128)} reshape(f32[16,4,4,64,64]{4,3,2,1,0:T(8,128)} %copy.35) | data formatting | bytes 8388608 | tf_op jit(solution)/shard_map/while/body/eval_jaxpr/reshape | solution.py:60
  344.5 8.3 %scatter_fusion = f32[128,4096]{1,0:T(8,128)S(1)} fusion(f32[128,4096]{1,0:T(8,128)S(1)} %get-tuple-element.167, s32[256]{0:T(256)S(1)} %bitcast.73, f32[256,4096]{1,0:T(8,128)} %reshape.191), kind=kCustom, calls=%fused_computation.2.clone.1 | custom fusion | flops 1048576 | bytes 12583936 | tf_op jit(solution)/shard_map/while/body/eval_jaxpr/scatter-add | solution.py:61
  364.0 6.1 %convolution_bitcast_fusion.2 = f32[16,4,4,64,64]{3,4,1,2,0:T(8,128)} fusion(bf16[16,128,4,64,1]{1,3,4,2,0:T(8,128)(2,1)} %bitcast.66, bf16[16,128,4,64]{1,3,2,0:T(8,128)(2,1)} %bitcast.67, pred[16]{0:T(512)(128)(4,1)S(1)} %get-tuple-element.156), kind=kOutput, calls=%fused_computation.3.clone.1 | convolution fusion | flops 268959744 | bytes 6291472 | tf_op jit(solution)/shard_map/while/body/eval_jaxpr/knta,knsb->ktsab/dot_general | solution.py:57
  370.1 9.3 %copy.35 = f32[16,4,4,64,64]{4,3,2,1,0:T(8,128)} copy(f32[16,4,4,64,64]{3,4,1,2,0:T(8,128)} %convolution_bitcast_fusion.2) | data formatting | bytes 8388608 | tf_op jit(solution)/shard_map/while/body/eval_jaxpr/knta,knsb->ktsab/transpose | solution.py:57
  379.4 7.9 %reshape.191 = f32[256,4096]{1,0:T(8,128)} reshape(f32[16,4,4,64,64]{4,3,2,1,0:T(8,128)} %copy.35) | data formatting | bytes 8388608 | tf_op jit(solution)/shard_map/while/body/eval_jaxpr/reshape | solution.py:60
  387.4 8.3 %scatter_fusion = f32[128,4096]{1,0:T(8,128)S(1)} fusion(f32[128,4096]{1,0:T(8,128)S(1)} %get-tuple-element.167, s32[256]{0:T(256)S(1)} %bitcast.73, f32[256,4096]{1,0:T(8,128)} %reshape.191), kind=kCustom, calls=%fused_computation.2.clone.1 | custom fusion | flops 1048576 | bytes 12583936 | tf_op jit(solution)/shard_map/while/body/eval_jaxpr/scatter-add | solution.py:61
  406.9 6.1 %convolution_bitcast_fusion.2 = f32[16,4,4,64,64]{3,4,1,2,0:T(8,128)} fusion(bf16[16,128,4,64,1]{1,3,4,2,0:T(8,128)(2,1)} %bitcast.66, bf16[16,128,4,64]{1,3,2,0:T(8,128)(2,1)} %bitcast.67, pred[16]{0:T(512)(128)(4,1)S(1)} %get-tuple-element.156), kind=kOutput, calls=%fused_computation.3.clone.1 | convolution fusion | flops 268959744 | bytes 6291472 | tf_op jit(solution)/shard_map/while/body/eval_jaxpr/knta,knsb->ktsab/dot_general | solution.py:57
  413.0 9.3 %copy.35 = f32[16,4,4,64,64]{4,3,2,1,0:T(8,128)} copy(f32[16,4,4,64,64]{3,4,1,2,0:T(8,128)} %convolution_bitcast_fusion.2) | data formatting | bytes 8388608 | tf_op jit(solution)/shard_map/while/body/eval_jaxpr/knta,knsb->ktsab/transpose | solution.py:57
  422.3 7.9 %reshape.191 = f32[256,4096]{1,0:T(8,128)} reshape(f32[16,4,4,64,64]{4,3,2,1,0:T(8,128)} %copy.35) | data formatting | bytes 8388608 | tf_op jit(solution)/shard_map/while/body/eval_jaxpr/reshape | solution.py:60
  430.3 8.3 %scatter_fusion = f32[128,4096]{1,0:T(8,128)S(1)} fusion(f32[128,4096]{1,0:T(8,128)S(1)} %get-tuple-element.167, s32[256]{0:T(256)S(1)} %bitcast.73, f32[256,4096]{1,0:T(8,128)} %reshape.191), kind=kCustom, calls=%fused_computation.2.clone.1 | custom fusion | flops 1048576 | bytes 12583936 | tf_op jit(solution)/shard_map/while/body/eval_jaxpr/scatter-add | solution.py:61
  438.6 32.8 %all_to_all.26 = f32[16,8,4096]{2,1,0:T(8,128)} all-to-all(f32[16,8,4096]{2,1,0:T(8,128)S(1)} %bitcast.65), channel_id=1, replica_groups=mesh['row'=32,'col'=16] {'col'}, dimensions={0} | all-to-all | bytes 4194304 | tf_op jit(solution)/shard_map/all_to_all | solution.py:35
  (92 shorter events, 73.3 us)
Async XLA Ops:
  6.5 82.4 %all-gather.2.cloned.1.call-start = ((), (), s32[]{:S(2)}) async-start(), calls=%async_computation.3 | async-start | bytes 4325376 | tf_op jit(solution)/shard_map/all_gather | solution.py:82
  89.0 57.2 %copy-start.1 = (bf16[2,128,256]{2,1,0:T(8,128)(2,1)S(1)}, bf16[2,128,256]{2,1,0:T(8,128)(2,1)}, u32[]{:S(2)}) copy-start(bf16[2,128,256]{2,1,0:T(8,128)(2,1)} %param.10) | copy-start | bytes 393220
  146.2 5.9 %copy-start.3 = (s32[1,1,96]{2,1,0:T(1,128)S(1)}, s32[1,1,96]{2,1,0:T(1,128)}, u32[]{:S(2)}) copy-start(s32[1,1,96]{2,1,0:T(1,128)} %param.9) | copy-start | bytes 1156
  146.2 6.6 %copy-start.4 = (s32[1,1,96]{2,1,0:T(1,128)S(1)}, s32[1,1,96]{2,1,0:T(1,128)}, u32[]{:S(2)}) copy-start(s32[1,1,96]{2,1,0:T(1,128)} %param.8) | copy-start | bytes 1156
  146.2 7.3 %copy-start.2 = (s32[1,1,96,4,4]{2,4,3,1,0:T(4,128)S(1)}, s32[1,1,96,4,4]{2,4,3,1,0:T(4,128)}, u32[]{:S(2)}) copy-start(s32[1,1,96,4,4]{2,4,3,1,0:T(4,128)} %param.11) | copy-start | bytes 18436
  147.8 32.0 %all-to-all-start.1 = ((bf16[16,2,128,256]{3,2,1,0:T(8,128)(2,1)}), bf16[16,2,128,256]{3,2,1,0:T(8,128)(2,1)S(1)}, u32[]{:S(2)}, u32[]{:S(2)}) async-start(bf16[16,2,128,256]{3,2,1,0:T(8,128)(2,1)} %broadcast_in_dim.32), calls=%async_computation.1 | async-start | bytes 4194304 | tf_op jit(solution)/shard_map/all_to_all | solution.py:11
  179.7 1.3 copy-start
Sparse Core Ops, SparseCore 0:
  9.5 79.4 all-gather.1
where the time goes:
time: 483 us; the launch traced here: 481 us
  local copies, waits for them, and re-layouts  164 us (34%)
  waiting for transfers between devices  104 us (22%)
  blocking collectives  90 us (19%)
  other arithmetic  53.6 us (11%)
  matrix products  51.7 us (11%)
  between operations  13.4 us (3%)
    all_gather x1, waiting for transfers between devices, on_device(): column_rows = lax.all_gather(p_blocks, 'row', axis=0, tiled=True)  81.7 us
    all_to_all x1, blocking collectives, on_device(): lax.all_to_all(grouped, 'col', split_axis=0, concat_axis=2, tiled=True)  57.2 us
    transpose x6, local copies, waits for them, and re-layouts, accumulate(): jnp.einsum('knta,knsb->ktsab', left_split, right_split, preferred_element...  55.5 us
    scatter-add x6, other arithmetic, accumulate(): running = running.at[sls.reshape(-1)].add(contribs)  49.7 us
    reshape x6, local copies, waits for them, and re-layouts, accumulate(): contribs.reshape(group_size * agg_blocks * agg_blocks, agg_width * agg_wi...  47.4 us
    dot_general x6, matrix products, accumulate(): jnp.einsum('knta,knsb->ktsab', left_split, right_split, preferred_element...  36.6 us
    all_to_all x1, blocking collectives, sum_at_owner(): lax.all_to_all(tiles, axis, split_axis=0, concat_axis=0, tiled=True)  32.8 us
    all_to_all x1, waiting for transfers between devices, copy_for_each(): lax.all_to_all(jnp.broadcast_to(array[None], (size, *array.shape)), axis,...  21.4 us
  transfers between devices with their start and end apart: 2, of which 2 were waited for; matrix products, arithmetic and copies ran while one was open for 1% of the time, Pallas kernels for 0%

commit v1 on v0

v1 whole, which is shorter than its diff:
```python
import functools

import jax
import jax.numpy as jnp
from jax import lax
from jax.experimental import pallas as pl
from jax.experimental.pallas import tpu as pltpu
from jax.sharding import PartitionSpec as P

MESH = pl.DeviceIdType.MESH
BF16, F32 = jnp.bfloat16, jnp.float32

HOP = 2
HALVES = 2


def gray(v):
    return v + v // 2 - 2 * ((v // 2) * (v % 2))


def panels_kernel(dims, p_ref, row_ref, col_ref, own_sem, send_sem, row_sem, z_send, z_recv, s_send, s_recv, c_sem):
    nz, ny, nx = dims
    ncol = ny * nx
    r, c = lax.axis_index("row"), lax.axis_index("col")
    z, core = r // 2, r % 2
    y, x = c // nx, c % nx
    up, down = 2 * ((z + 1) % nz) + core, 2 * ((z + nz - 1) % nz) + core
    sibling = 2 * z + 1 - core
    half = p_ref.shape[1] // HALVES
    base = core * 2 * ncol
    steps_x = [gray(v) for v in range(1, nx)]
    steps_y = [gray(v) for v in range(1, ny)]

    def along_x(d):
        return y * nx + (x + d) % nx

    def along_y(d):
        return ((y + d) % ny) * nx + x

    barrier = pltpu.get_barrier_semaphore()
    peers = [(r, along_x(d)) for d in steps_x] + [(r, along_y(d)) for d in steps_y]
    peers += [(up, c), (down, c), (sibling, c)]
    for peer in peers:
        pl.semaphore_signal(barrier, inc=1, device_id=peer, device_id_type=MESH)
    pl.semaphore_wait(barrier, len(peers))

    def row_copy(src, row, slot, target):
        return pltpu.make_async_remote_copy(
            src_ref=src,
            dst_ref=row_ref.at[row],
            send_sem=send_sem.at[slot],
            recv_sem=row_sem.at[row],
            device_id=(r, target),
            device_id_type=MESH,
        )

    sends = []

    def give(src, row, target):
        copy = row_copy(src, row, len(sends), target)
        copy.start()
        sends.append(copy)

    def arrived(row):
        row_copy(row_ref.at[row], row, 0, c).wait_recv()

    hops_up, hops_down = (z - c + nz) % nz, (c - z + nz) % nz
    root = hops_up == 0
    count = ncol * HALVES

    def row_up(q):
        u, v = gray(q // nx), gray(q % nx)
        return 2 * (((y + u) % ny) * nx + (x + v) % nx)

    def row_down(q):
        u, v = gray(q // ny), gray(q % ny)
        return 2 * (((y + v) % ny) * nx + (x + u) % nx) + 1

    def part(ref, row, h):
        return ref.at[row, pl.ds(pl.multiple_of(h * half, half), half)]

    def place(way, n):
        q, h = n // HALVES, n % HALVES
        return (row_up(q) if way == 0 else row_down(q)), h

    def z_copy(way, n, from_root):
        row, h = place(way, n)
        return pltpu.make_async_remote_copy(
            src_ref=part(row_ref, row, h) if from_root else part(col_ref, base + row, h),
            dst_ref=part(col_ref, base + row, h),
            send_sem=z_send.at[way, n],
            recv_sem=z_recv.at[way, n],
            device_id=(up if way == 0 else down, c),
            device_id_type=MESH,
        )

    def s_copy(way, n, from_root):
        row, h = place(way, n)
        return pltpu.make_async_remote_copy(
            src_ref=part(row_ref, row, h) if from_root else part(col_ref, base + row, h),
            dst_ref=part(col_ref, base + row, h),
            send_sem=s_send.at[way, n],
            recv_sem=s_recv.at[way, n],
            device_id=(sibling, c),
            device_id_type=MESH,
        )

    def c_copy(way, n):
        row, h = place(way, n)
        return pltpu.make_async_copy(part(row_ref, row, h), part(col_ref, base + row, h), c_sem.at[way, n])

    def from_root(way, n):
        z_copy(way, n, True).start()
        s_copy(way, n, True).start()
        c_copy(way, n).start()

    def relay(way, n):
        hops = hops_up if way == 0 else hops_down

        @pl.when(root & (n >= HALVES))
        def _():
            @pl.when((n % HALVES == 0) & (n >= HALVES * (nx if way == 0 else ny)))
            def _():
                arrived(place(way, n)[0])

            from_root(way, n)

        @pl.when(jnp.logical_not(root))
        def _():
            z_copy(way, n, False).wait_recv()

            @pl.when(hops < nz - 1)
            def _():
                z_copy(way, n, False).start()

            s_copy(way, n, False).start()

    mine = pltpu.make_async_copy(p_ref, row_ref.at[pl.ds(2 * c, 2)], own_sem)
    mine.start()
    for i in range(max(nx, ny) - 1):
        if i < nx - 1:
            give(p_ref.at[0], 2 * c, along_x(steps_x[i]))
        if i < ny - 1:
            give(p_ref.at[1], 2 * c + 1, along_y(steps_y[i]))
    mine.wait()

    @pl.when(root)
    def _():
        for n in range(HALVES):
            from_root(0, n)
            from_root(1, n)

    for d in steps_y:
        give(p_ref.at[0], 2 * c, along_y(d))
    for d in steps_x:
        give(p_ref.at[1], 2 * c + 1, along_x(d))
    for i in range(max(nx, ny) - 1):
        if i < nx - 1:
            row = 2 * along_x(steps_x[i])
            arrived(row)
            for d in steps_y:
                give(row_ref.at[row], row, along_y(d))
        if i < ny - 1:
            row = 2 * along_y(steps_y[i]) + 1
            arrived(row)
            for d in steps_x:
                give(row_ref.at[row], row, along_x(d))

    @pl.loop(0, count + HOP * (nz - 1))
    def _(step):
        n_up, n_down = step - HOP * hops_up, step - HOP * hops_down

        @pl.when((n_up >= 0) & (n_up < count))
        def _():
            relay(0, n_up)

        @pl.when((n_down >= 0) & (n_down < count))
        def _():
            relay(1, n_down)

    @pl.when(jnp.logical_not(root))
    def _():
        @pl.loop(nx, ncol)
        def _(q):
            arrived(row_up(q))

        @pl.loop(ny, ncol)
        def _(q):
            arrived(row_down(q))

    for copy in sends:
        copy.wait_send()

    @pl.loop(0, count)
    def _(n):
        for way, hops in ((0, hops_up), (1, hops_down)):
            @pl.when(hops < nz - 1)
            def _():
                z_copy(way, n, False).wait_send()

            s_copy(way, n, False).wait_send()
            s_copy(way, n, False).wait_recv()

            @pl.when(root)
            def _():
                c_copy(way, n).wait()


def panels(p_blocks, dims):
    nz, ny, nx = dims
    ncol = ny * nx
    _, node, width = p_blocks.shape
    count = ncol * HALVES
    vmem = pl.BlockSpec(memory_space=pltpu.VMEM)
    dma = pltpu.SemaphoreType.DMA
    return pl.pallas_call(
        functools.partial(panels_kernel, dims),
        out_shape=(
            jax.ShapeDtypeStruct((2 * ncol, node, width), BF16),
            jax.ShapeDtypeStruct((4 * ncol, node, width), BF16),
        ),
        in_specs=[vmem],
        out_specs=(vmem, vmem),
        scratch_shapes=[
            dma,
            dma((2 * (ncol - 1),)),
            dma((2 * ncol,)),
            dma((2, count)),
            dma((2, count)),
            dma((2, count)),
            dma((2, count)),
            dma((2, count)),
        ],
        compiler_params=pltpu.CompilerParams(collective_id=0, has_side_effects=True, vmem_limit_bytes=24 << 20),
        name="panels",
    )(p_blocks)


GROUP = 4


def terms_kernel(rows_ref, cols_ref, slots_ref, a_ref, row_ref, col_ref, out_ref, left, *totals):
    count = a_ref.shape[0]
    panel_rows, node, width = row_ref.shape
    kp = len(totals)
    agg = width // kp
    half = agg // 2

    for total in totals:
        total[...] = jnp.zeros_like(total)

    to = lax.broadcasted_iota(jnp.int32, (width, width), 0)
    at = lax.broadcasted_iota(jnp.int32, (width, width), 1)
    inner = to % agg
    source = to - inner + 2 * (inner % half) + inner // half
    pick = jnp.where(at == source, 1.0, 0.0).astype(BF16)

    @pl.loop(0, panel_rows, unroll=2)
    def _(i):
        left[i] = lax.dot_general(
            pick, row_ref[i], (((1,), (1,)), ((), ())), preferred_element_type=F32
        ).astype(BF16)

    low = lax.broadcasted_iota(jnp.int32, (half, 2 * agg), 1) < agg

    def block(k):
        product = jnp.dot(a_ref[k], col_ref[cols_ref[k]], preferred_element_type=F32).astype(BF16)
        term = jnp.dot(left[rows_ref[k]], product, preferred_element_type=F32)
        for pair in range(kp // 2):
            lanes = slice(pair * 2 * agg, (pair + 1) * 2 * agg)
            for t in range(kp):
                even = term[t * agg : t * agg + half, lanes]
                odd = term[t * agg + half : (t + 1) * agg, lanes]
                total = totals[t]
                slot = slots_ref[(k * kp + t) * kp + 2 * pair]
                total[slot] += jnp.where(low, even, pltpu.roll(odd, agg, 1))
                slot = slots_ref[(k * kp + t) * kp + 2 * pair + 1]
                total[slot] += jnp.where(low, pltpu.roll(even, agg, 1), odd)

    @pl.loop(0, count // GROUP)
    def _(g):
        for i in range(GROUP):
            block(g * GROUP + i)

    @pl.loop(0, out_ref.shape[0] // 8)
    def _(g):
        some = pl.ds(pl.multiple_of(g * 8, 8), 8)
        out_ref[some] = functools.reduce(lambda p, q: p + q, [total[some] for total in totals]).astype(BF16)


def local_terms(a_blocks, a_rows, a_cols, slots, row_panel, col_panel, slot_count):
    panel_rows, node, width = row_panel.shape
    kp = slots.shape[1]
    agg = width // kp
    vmem, smem = pl.BlockSpec(memory_space=pltpu.VMEM), pl.BlockSpec(memory_space=pltpu.SMEM)
    return pl.pallas_call(
        terms_kernel,
        out_shape=jax.ShapeDtypeStruct((slot_count, agg // 2, 2 * agg), BF16),
        in_specs=[smem, smem, smem, vmem, vmem, vmem],
        out_specs=vmem,
        scratch_shapes=[pltpu.VMEM((panel_rows, width, node), BF16)]
        + [pltpu.VMEM((slot_count, agg // 2, 2 * agg), F32)] * kp,
        compiler_params=pltpu.CompilerParams(vmem_limit_bytes=48 << 20),
        name="terms",
    )(a_rows, a_cols, slots.reshape(-1), a_blocks, row_panel, col_panel)


def sums_kernel(ncol, part_ref, out_ref, landed, own_sem, send_sem, recv_sem):
    r, c = lax.axis_index("row"), lax.axis_index("col")
    share = out_ref.shape[0]
    barrier = pltpu.get_barrier_semaphore()
    for d in range(1, ncol):
        pl.semaphore_signal(barrier, inc=1, device_id=(r, (c + d) % ncol), device_id_type=MESH)
    pl.semaphore_wait(barrier, ncol - 1)

    def copy(d):
        target = (c + d) % ncol
        return pltpu.make_async_remote_copy(
            src_ref=part_ref.at[pl.ds(target * share, share)],
            dst_ref=landed.at[d],
            send_sem=send_sem.at[d],
            recv_sem=recv_sem.at[d],
            device_id=(r, target),
            device_id_type=MESH,
        )

    for d in range(1, ncol):
        copy(d).start()
    mine = pltpu.make_async_copy(part_ref.at[pl.ds(c * share, share)], landed.at[0], own_sem)
    mine.start()
    mine.wait()
    for d in range(1, ncol):
        copy(d).wait_recv()
    for d in range(1, ncol):
        copy(d).wait_send()
    rows, lanes = landed.shape[2:]
    total = landed[0].astype(F32)
    for d in range(1, ncol):
        total = total + landed[d].astype(F32)
    for i in range(rows):
        out_ref[:, i * lanes : (i + 1) * lanes] = total[:, i, :].astype(BF16)


def sum_at_owner(partial, ncol):
    slots, rows, lanes = partial.shape
    share = slots // ncol
    vmem = pl.BlockSpec(memory_space=pltpu.VMEM)
    dma = pltpu.SemaphoreType.DMA
    return pl.pallas_call(
        functools.partial(sums_kernel, ncol),
        out_shape=jax.ShapeDtypeStruct((share, rows * lanes), BF16),
        in_specs=[vmem],
        out_specs=vmem,
        scratch_shapes=[
            pltpu.VMEM((ncol, share, rows, lanes), BF16),
            dma,
            dma((ncol,)),
            dma((ncol,)),
        ],
        compiler_params=pltpu.CompilerParams(collective_id=1, has_side_effects=True, vmem_limit_bytes=16 << 20),
        name="sums",
    )(partial)


def on_device(dims, slot_count, a_blocks, a_rows, a_cols, p_blocks, coarse_slot):
    ncol = dims[1] * dims[2]
    row_panel, col_panel = panels(p_blocks, dims)
    partial = local_terms(
        a_blocks[0, 0], a_rows[0, 0], a_cols[0, 0], coarse_slot[0, 0], row_panel, col_panel, slot_count
    )
    return sum_at_owner(partial, ncol)[None]


def solution(mesh, dims=(16, 4, 4), slot_count=128):
    placed = (
        P("row", "col", None, None, None),
        P("row", "col", None),
        P("row", "col", None),
        P(("row", "col"), None, None),
        P("row", "col", None, None, None),
    )
    return jax.shard_map(
        functools.partial(on_device, dims, slot_count),
        mesh=mesh,
        in_specs=placed,
        out_specs=P("row", "col", None),
        check_vma=False,
    )
```

time: 483 us -> 166 us (0.34)
  Pallas kernels: 0 us -> 160 us
  local copies, waits for them, and re-layouts: 164 us -> 5.82 us
  waiting for transfers between devices: 104 us -> 0 us
  blocking collectives: 90 us -> 0 us
  other arithmetic: 53.6 us -> 0 us
  matrix products: 51.7 us -> 0 us
  between operations: 13.4 us -> 0.05 us
    pallas_call x0 -> x3, Pallas kernels: none -> 160 us  [the longest x1 93.7 us: sum_at_owner(): pl.pallas_call(functools.partial(sums_kernel, ncol), out_shape=jax.ShapeD...]
    all_to_all x2 -> x0, blocking collectives: 90 us -> none  [the longest x1 57.2 us: on_device(): lax.all_to_all(grouped, 'col', split_axis=0, concat_axis=2, tiled=True)]
    all_gather x1 -> x0, waiting for transfers between devices: 81.7 us -> none  [on_device(): column_rows = lax.all_gather(p_blocks, 'row', axis=0, tiled=True)]
    transpose x6 -> x0, local copies, waits for them, and re-layouts: 55.5 us -> none  [accumulate(): jnp.einsum('knta,knsb->ktsab', left_split, right_split, preferred_element...]
    dot_general x12 -> x0, matrix products: 51.7 us -> none  [the longest x6 36.6 us: accumulate(): jnp.einsum('knta,knsb->ktsab', left_split, right_split, preferred_element...]
    scatter-add x6 -> x0, other arithmetic: 49.7 us -> none  [accumulate(): running = running.at[sls.reshape(-1)].add(contribs)]
    reshape x12 -> x0, local copies, waits for them, and re-layouts: 48 us -> none  [the longest x6 47.4 us: accumulate(): contribs.reshape(group_size * agg_blocks * agg_blocks, agg_width * agg_wi...]
    gather x18 -> x0, local copies, waits for them, and re-layouts: 37.8 us -> none  [the longest x12 21 us: accumulate(): left_rows = jnp.take(row_panel, rws, axis=0)]
  transfers between devices with their start and end apart: 2 -> 0, of which waited for: 2 -> 0; matrix products, arithmetic and copies ran while one was open for 1% -> 0% of each run, Pallas kernels for 0% -> 0%
where the time goes in v1:
time: 166 us
  Pallas kernels  160 us (96%)
  local copies, waits for them, and re-layouts  5.82 us (4%)
    pallas_call x1, Pallas kernels, sum_at_owner(): pl.pallas_call(functools.partial(sums_kernel, ncol), out_shape=jax.ShapeD...  93.7 us
    pallas_call x1, Pallas kernels, panels(): pl.pallas_call(functools.partial(panels_kernel, dims), out_shape=(jax.Sha...  40.6 us
    pallas_call x1, Pallas kernels, local_terms(): pl.pallas_call(terms_kernel, out_shape=jax.ShapeDtypeStruct((slot_count,...  26.1 us
    unnamed x10, local copies, waits for them, and re-layouts  5.61 us

profile of v1, /device:TPU:1, one launch (start us, length us, event | category | flops | bytes accessed | tf_op | source)
XLA Modules:
  0.0 166.2 jit_solution(13495810999599881890)
XLA Ops:
  0.0 0.8 copy.6
  0.8 0.2 reshape_squeeze.3.slots_ref
  1.1 0.0 copy-start.1
  1.1 0.9 copy-done.1
  2.0 40.6 %panels.1 = (bf16[32,128,256]{2,1,0:T(8,128)(2,1)S(1)}, bf16[64,128,256]{2,1,0:T(8,128)(2,1)S(1)}) custom-call(bf16[2,128,256]{2,1,0:T(8,128)(2,1)S(1)} %copy-done.1), custom_call_target="tpu_custom_call" | custom-call | tf_op jit(solution)/shard_map/panels/pallas_call | solution.py:216
  42.5 0.0 copy-start
  42.6 1.9 %copy-done = bf16[64,128,256]{2,1,0:T(8,128)(2,1)} copy-done((bf16[64,128,256]{2,1,0:T(8,128)(2,1)}, bf16[64,128,256]{2,1,0:T(8,128)(2,1)S(1)}, u32[]{:S(2)}) %copy-start) | copy-done | bytes 4194328
  44.5 0.0 copy-start.2
  44.5 0.7 copy-done.2
  45.1 0.0 copy-start.3
  45.1 0.7 copy-done.3
  45.8 26.1 %terms.1.part_ref = bf16[128,32,128]{2,1,0:T(8,128)(2,1)S(1)} custom-call(s32[96]{0:T(128)S(1)} %bitcast.5, s32[96]{0:T(128)S(1)} %bitcast.6, s32[1536]{0:T(1024)S(1)} %reshape_squeeze.3.slots_ref, bf16[96,128,128]{2,1,0:T(8,128)(2,1)} %bitcast.7, bf16[32,128,256]{2,1,0:T(8,128)(2,1)S(1)} %get-tuple-element.7.row_ref, bf16[64,128,256]{2,1,0:T(8,128)(2,1)} %copy-done), custom_call_target="tpu_custom_call" | custom-call | tf_op jit(solution)/shard_map/terms/pallas_call | solution.py:296
  71.9 93.7 %sums.1 = bf16[8,4096]{1,0:T(8,128)(2,1)S(1)} custom-call(bf16[128,32,128]{2,1,0:T(8,128)(2,1)S(1)} %terms.1.part_ref), custom_call_target="tpu_custom_call" | custom-call | tf_op jit(solution)/shard_map/sums/pallas_call | solution.py:349
  165.6 0.6 copy.8
Async XLA Ops:
  1.1 0.9 copy-start.1
  42.5 1.9 %copy-start = (bf16[64,128,256]{2,1,0:T(8,128)(2,1)}, bf16[64,128,256]{2,1,0:T(8,128)(2,1)S(1)}, u32[]{:S(2)}) copy-start(bf16[64,128,256]{2,1,0:T(8,128)(2,1)S(1)} %get-tuple-element.8.col_ref) | copy-start | bytes 12582916
  44.5 0.7 copy-start.2
  45.1 0.7 copy-start.3

commit v2 on v1

v2 whole, which is shorter than its diff:
```python
import functools

import jax
import jax.numpy as jnp
from jax import lax
from jax.experimental import pallas as pl
from jax.experimental.pallas import tpu as pltpu
from jax.sharding import PartitionSpec as P

MESH = pl.DeviceIdType.MESH
BF16, F32 = jnp.bfloat16, jnp.float32

HOP = 4
KP = 4
GROUP = 16
PARTS = 2


def gray(v):
    return v + v // 2 - 2 * ((v // 2) * (v % 2))


def panels_kernel(dims, p_ref, row_ref, col_ref, passing, own_sem, g_send, g_recv, r_send, r_recv, z_send, z_recv, a_send, a_recv, s_send, s_recv):
    nz, ny, nx = dims
    ncol = ny * nx
    r, c = lax.axis_index("row"), lax.axis_index("col")
    z, core = r // 2, r % 2
    y, x = c // nx, c % nx
    up, down = 2 * ((z + 1) % nz) + core, 2 * ((z + nz - 1) % nz) + core
    sibling = 2 * z + 1 - core
    base = core * 2 * ncol
    far = nz // 2
    steps_x = [gray(v) for v in range(1, nx)]
    steps_y = [gray(v) for v in range(1, ny)]

    def along_x(d):
        return y * nx + (x + d) % nx

    def along_y(d):
        return ((y + d) % ny) * nx + x

    barrier = pltpu.get_barrier_semaphore()
    peers = [(r, along_x(d)) for d in steps_x] + [(r, along_y(d)) for d in steps_y]
    peers += [(up, c), (down, c), (sibling, c)]
    for peer in peers:
        pl.semaphore_signal(barrier, inc=1, device_id=peer, device_id_type=MESH)
    pl.semaphore_wait(barrier, len(peers))

    def remote(src, dst, send, recv, device):
        return pltpu.make_async_remote_copy(
            src_ref=src, dst_ref=dst, send_sem=send, recv_sem=recv, device_id=device, device_id_type=MESH
        )

    root = x == z % nx
    plane = z // nx

    def gather_copy(x0):
        return remote(p_ref, passing.at[plane, x0], g_send, g_recv.at[x0], (r, y * nx + z % nx))

    part = p_ref.shape[1] // PARTS

    def z_copy(way, y1, x0, j):
        here = passing.at[y1, x0, j // PARTS, pl.ds(pl.multiple_of(j % PARTS * part, part), part)]
        return remote(here, here, z_send.at[way, y1, x0, j], z_recv.at[way, y1, x0, j], (up if way == 0 else down, c))

    def name(way, pos):
        o = pos if way == 0 else (nx - pos) % nx
        return (x + o) % nx, (o < nx // 2 if way == 0 else o >= nx // 2)

    def a_copy(y1, x0):
        rows = col_ref.at[pl.ds(base + 2 * (y * nx + x0), 2)]
        return remote(passing.at[y1, x0], rows, a_send.at[y1, x0], a_recv.at[y * nx + x0], (r, y1 * nx + x))

    def deliver(y1, x0):
        @pl.when(y1 != y)
        def _():
            a_copy(y1, x0).start()

        @pl.when(y1 == y)
        def _():
            rows = col_ref.at[pl.ds(base + 2 * (y * nx + x0), 2)]
            pltpu.make_async_copy(passing.at[y1, x0], rows, a_recv.at[y * nx + x0]).start()

    sends = []

    def give(src, piece, target):
        rows = row_ref.at[pl.ds(2 * piece, 2)]
        copy = remote(src, rows, r_send.at[len(sends)], r_recv.at[piece], (r, target))
        copy.start()
        sends.append(copy)

    def arrived(piece):
        rows = row_ref.at[pl.ds(2 * piece, 2)]
        remote(rows, rows, r_send.at[0], r_recv.at[piece], (r, c)).wait_recv()

    @pl.when(jnp.logical_not(root))
    def _():
        gather_copy(x).start()

    @pl.when(root)
    def _():
        copy = pltpu.make_async_copy(p_ref, passing.at[plane, x], own_sem.at[1])
        copy.start()
        copy.wait()
        for j in range(2 * PARTS):
            z_copy(0, plane, x, j).start()
            z_copy(1, plane, x, j).start()
        deliver(plane, x)

    mine = pltpu.make_async_copy(p_ref, row_ref.at[pl.ds(2 * c, 2)], own_sem.at[0])
    mine.start()
    for d in steps_y:
        give(p_ref, c, along_y(d))
    for d in steps_x:
        give(p_ref, c, along_x(d))

    @pl.when(root)
    def _():
        for pos in range(1, nx):
            a, b = name(0, pos)[0], name(1, pos)[0]
            if 2 * pos <= nx:
                gather_copy(a).wait_recv()
                if 2 * pos < nx:
                    gather_copy(b).wait_recv()
            for j in range(2 * PARTS):
                z_copy(0, plane, a, j).start()
                z_copy(1, plane, b, j).start()
            deliver(plane, a)

    for d in steps_y:
        piece = along_y(d)
        arrived(piece)
        for e in steps_x:
            give(row_ref.at[pl.ds(2 * piece, 2)], piece, along_x(e))

    near_up = (z - x + nz - 1) % nx + 1
    near_down = (x - z + nz - 1) % nx + 1
    feeds, parts = far // nx, 2 * PARTS
    chunks = nx * parts

    def chunk(way, feed, n):
        dist = (near_up if way == 0 else near_down) + nx * feed
        z0 = (z - dist + nz) % nz if way == 0 else (z + dist) % nz
        x0, opposite = name(way, n // parts)
        comes = (dist < far) | ((dist == far) & opposite)
        goes = (dist < far - 1) | ((dist == far - 1) & opposite)
        return z0 // nx, x0, n % parts, comes, goes

    def relay(way, feed, n):
        y1, x0, j, comes, goes = chunk(way, feed, n)

        @pl.when(comes)
        def _():
            z_copy(way, y1, x0, j).wait_recv()

            @pl.when(goes)
            def _():
                z_copy(way, y1, x0, j).start()

            @pl.when(j == parts - 1)
            def _():
                deliver(y1, x0)

    @pl.loop(0, chunks + HOP * (far - 1))
    def _(step):
        for feed in range(feeds):
            for way, near in ((0, near_up), (1, near_down)):
                n = step - HOP * (near + nx * feed - 1)

                @pl.when((n >= 0) & (n < chunks))
                def _():
                    relay(way, feed, n)

    def s_copy(c0):
        rows = col_ref.at[pl.ds(base + 2 * c0, 2)]
        return remote(rows, rows, s_send.at[c0], s_recv.at[c0], (sibling, c))

    @pl.loop(0, ncol)
    def _(i):
        c0 = (c + i) % ncol
        rows = col_ref.at[pl.ds(base + 2 * c0, 2)]
        remote(passing.at[0, 0], rows, a_send.at[0, 0], a_recv.at[c0], (r, c)).wait_recv()
        s_copy(c0).start()

    for u in range(ny):
        for v in range(1, nx):
            arrived(((y + u) % ny) * nx + (x + v) % nx)
    mine.wait()
    for copy in sends:
        copy.wait_send()

    @pl.when(jnp.logical_not(root))
    def _():
        gather_copy(x).wait_send()

    @pl.loop(0, nx)
    def _(x0):
        @pl.when(root)
        def _():
            for j in range(2 * PARTS):
                z_copy(0, plane, x0, j).wait_send()
                z_copy(1, plane, x0, j).wait_send()

        for y1 in range(ny):
            @pl.when(y1 != y)
            def _():
                a_copy(y1, x0).wait_send()

    @pl.loop(0, chunks)
    def _(n):
        for feed in range(feeds):
            for way in (0, 1):
                y1, x0, j, comes, goes = chunk(way, feed, n)

                @pl.when(comes & goes)
                def _():
                    z_copy(way, y1, x0, j).wait_send()

    @pl.loop(0, ncol)
    def _(c0):
        s_copy(c0).wait_send()
        s_copy(c0).wait_recv()


def panels(p_blocks, dims):
    nz, ny, nx = dims
    ncol = ny * nx
    _, node, width = p_blocks.shape
    vmem = pl.BlockSpec(memory_space=pltpu.VMEM)
    dma = pltpu.SemaphoreType.DMA
    return pl.pallas_call(
        functools.partial(panels_kernel, dims),
        out_shape=(
            jax.ShapeDtypeStruct((2 * ncol, node, width), BF16),
            jax.ShapeDtypeStruct((4 * ncol, node, width), BF16),
        ),
        in_specs=[vmem],
        out_specs=(vmem, vmem),
        scratch_shapes=[
            pltpu.VMEM((ny, nx, 2, node, width), BF16),
            dma((2,)),
            dma,
            dma((nx,)),
            dma((ncol - 1,)),
            dma((ncol,)),
            dma((2, ny, nx, 2 * PARTS)),
            dma((2, ny, nx, 2 * PARTS)),
            dma((ny, nx)),
            dma((ncol,)),
            dma((ncol,)),
            dma((ncol,)),
        ],
        compiler_params=pltpu.CompilerParams(collective_id=0, has_side_effects=True, vmem_limit_bytes=16 << 20),
        name="panels",
    )(p_blocks)


def terms_kernel(rows_ref, cols_ref, slots_ref, a_ref, row_ref, col_ref, out_ref, turned, left_ref, *totals):
    count, width, node = left_ref.shape
    panel_rows = row_ref.shape[0]
    agg = width // KP
    half = agg // 2

    @pl.loop(0, out_ref.shape[0] // 8)
    def _(g):
        some = pl.ds(pl.multiple_of(g * 8, 8), 8)
        for total in totals:
            total[some] = jnp.zeros((8, *total.shape[1:]), F32)

    to = lax.broadcasted_iota(jnp.int32, (width, width), 0)
    at = lax.broadcasted_iota(jnp.int32, (width, width), 1)
    inner = to % agg
    source = to - inner + 2 * (inner % half) + inner // half
    pick = jnp.where(at == source, 1.0, 0.0).astype(BF16)

    @pl.loop(0, panel_rows // 8)
    def _(g):
        for i in range(8):
            turned[g * 8 + i] = lax.dot_general(
                pick, row_ref[g * 8 + i], (((1,), (1,)), ((), ())), preferred_element_type=F32
            ).astype(BF16)

    @pl.loop(0, count // GROUP)
    def _(g):
        for i in range(GROUP):
            k = g * GROUP + i
            left_ref[k] = jnp.dot(turned[rows_ref[k]], a_ref[k], preferred_element_type=F32).astype(BF16)

    low = lax.broadcasted_iota(jnp.int32, (half, 2 * agg), 1) < agg

    def block(k):
        term = jnp.dot(left_ref[k], col_ref[cols_ref[k]], preferred_element_type=F32)
        for pair in range(KP // 2):
            lanes = slice(pair * 2 * agg, (pair + 1) * 2 * agg)
            for t in range(KP):
                even = term[t * agg : t * agg + half, lanes]
                odd = term[t * agg + half : (t + 1) * agg, lanes]
                total = totals[t % len(totals)]
                total[slots_ref[t, 2 * pair, k]] += jnp.where(low, even, pltpu.roll(odd, agg, 1))
                total[slots_ref[t, 2 * pair + 1, k]] += jnp.where(low, pltpu.roll(even, agg, 1), odd)

    @pl.loop(0, count // GROUP)
    def _(g):
        for i in range(GROUP):
            block(g * GROUP + i)

    @pl.loop(0, out_ref.shape[0] // 8)
    def _(g):
        some = pl.ds(pl.multiple_of(g * 8, 8), 8)
        out_ref[some] = functools.reduce(lambda p, q: p + q, [total[some] for total in totals]).astype(BF16)


def local_terms(a_blocks, a_rows, a_cols, slots, row_panel, col_panel, slot_count):
    count = a_blocks.shape[0]
    panel_rows, node, width = row_panel.shape
    agg = width // KP
    vmem, smem = pl.BlockSpec(memory_space=pltpu.VMEM), pl.BlockSpec(memory_space=pltpu.SMEM)
    return pl.pallas_call(
        functools.partial(terms_kernel),
        out_shape=jax.ShapeDtypeStruct((slot_count, agg // 2, 2 * agg), BF16),
        in_specs=[smem, smem, smem, vmem, vmem, vmem],
        out_specs=vmem,
        scratch_shapes=[pltpu.VMEM((panel_rows, width, node), BF16), pltpu.VMEM((count, width, node), BF16)]
        + [pltpu.VMEM((slot_count, agg // 2, 2 * agg), F32)] * 2,
        compiler_params=pltpu.CompilerParams(vmem_limit_bytes=36 << 20),
        name="terms",
    )(a_rows, a_cols, jnp.transpose(slots, (1, 2, 0)), a_blocks, row_panel, col_panel)


def sums_kernel(ncol, part_ref, out_ref, landed, own_sem, send_sem, recv_sem):
    r, c = lax.axis_index("row"), lax.axis_index("col")
    share = out_ref.shape[0]
    barrier = pltpu.get_barrier_semaphore()
    for d in range(1, ncol):
        pl.semaphore_signal(barrier, inc=1, device_id=(r, (c + d) % ncol), device_id_type=MESH)
    pl.semaphore_wait(barrier, ncol - 1)

    def copy(d):
        target = (c + d) % ncol
        return pltpu.make_async_remote_copy(
            src_ref=part_ref.at[pl.ds(target * share, share)],
            dst_ref=landed.at[d],
            send_sem=send_sem.at[d],
            recv_sem=recv_sem.at[d],
            device_id=(r, target),
            device_id_type=MESH,
        )

    for d in range(1, ncol):
        copy(d).start()
    mine = pltpu.make_async_copy(part_ref.at[pl.ds(c * share, share)], landed.at[0], own_sem)
    mine.start()
    mine.wait()
    for d in range(1, ncol):
        copy(d).wait_recv()
    for d in range(1, ncol):
        copy(d).wait_send()
    rows, lanes = landed.shape[2:]
    total = landed[0].astype(F32)
    for d in range(1, ncol):
        total = total + landed[d].astype(F32)
    for i in range(rows):
        out_ref[:, i * lanes : (i + 1) * lanes] = total[:, i, :].astype(BF16)


def sum_at_owner(partial, ncol):
    slots, rows, lanes = partial.shape
    share = slots // ncol
    vmem = pl.BlockSpec(memory_space=pltpu.VMEM)
    dma = pltpu.SemaphoreType.DMA
    return pl.pallas_call(
        functools.partial(sums_kernel, ncol),
        out_shape=jax.ShapeDtypeStruct((share, rows * lanes), BF16),
        in_specs=[vmem],
        out_specs=vmem,
        scratch_shapes=[
            pltpu.VMEM((ncol, share, rows, lanes), BF16),
            dma,
            dma((ncol,)),
            dma((ncol,)),
        ],
        compiler_params=pltpu.CompilerParams(collective_id=1, has_side_effects=True, vmem_limit_bytes=16 << 20),
        name="sums",
    )(partial)


def on_device(dims, slot_count, a_blocks, a_rows, a_cols, p_blocks, coarse_slot):
    ncol = dims[1] * dims[2]
    row_panel, col_panel = panels(p_blocks, dims)
    partial = local_terms(
        a_blocks[0, 0], a_rows[0, 0], a_cols[0, 0], coarse_slot[0, 0], row_panel, col_panel, slot_count
    )
    return sum_at_owner(partial, ncol)[None]


def solution(mesh, dims=(16, 4, 4), slot_count=128):
    placed = (
        P("row", "col", None, None, None),
        P("row", "col", None),
        P("row", "col", None),
        P(("row", "col"), None, None),
        P("row", "col", None, None, None),
    )
    return jax.shard_map(
        functools.partial(on_device, dims, slot_count),
        mesh=mesh,
        in_specs=placed,
        out_specs=P("row", "col", None),
        check_vma=False,
    )
```

time: 166 us -> 111 us (0.67)
  Pallas kernels: 160 us -> 105 us
    pallas_call x1, Pallas kernels: 93.7 us -> 28.9 us  [sum_at_owner(): pl.pallas_call(functools.partial(sums_kernel, ncol), out_shape=jax.ShapeD...]
    pallas_call x1, Pallas kernels: 40.6 us -> 62.9 us  [panels(): pl.pallas_call(functools.partial(panels_kernel, dims), out_shape=(jax.Sha...]
    pallas_call x1, Pallas kernels: 26.1 us -> 13.6 us  [local_terms(): pl.pallas_call(functools.partial(terms_kernel), out_shape=jax.ShapeDtypeS...]
    unnamed x10 -> x11, local copies, waits for them, and re-layouts: 5.61 us -> 5.43 us
where the time goes in v2:
time: 111 us
  Pallas kernels  105 us (95%)
  local copies, waits for them, and re-layouts  5.43 us (5%)
    pallas_call x1, Pallas kernels, panels(): pl.pallas_call(functools.partial(panels_kernel, dims), out_shape=(jax.Sha...  62.9 us
    pallas_call x1, Pallas kernels, sum_at_owner(): pl.pallas_call(functools.partial(sums_kernel, ncol), out_shape=jax.ShapeD...  28.9 us
    pallas_call x1, Pallas kernels, local_terms(): pl.pallas_call(functools.partial(terms_kernel), out_shape=jax.ShapeDtypeS...  13.6 us
    unnamed x11, local copies, waits for them, and re-layouts  5.43 us

profile of v2, /device:TPU:1, one launch (start us, length us, event | category | flops | bytes accessed | tf_op | source)
XLA Modules:
  0.0 110.8 jit_solution(11136571685243957408)
XLA Ops:
  0.0 0.0 copy-start.1
  0.0 0.9 copy-done.1
  0.9 62.9 %panels.1 = (bf16[32,128,256]{2,1,0:T(8,128)(2,1)S(1)}, bf16[64,128,256]{2,1,0:T(8,128)(2,1)S(1)}) custom-call(bf16[2,128,256]{2,1,0:T(8,128)(2,1)S(1)} %copy-done.1), custom_call_target="tpu_custom_call" | custom-call | tf_op jit(solution)/shard_map/panels/pallas_call | solution.py:231
  63.8 0.0 copy-start
  63.8 1.9 %copy-done = bf16[1,1,96,128,128]{4,3,2,1,0:T(8,128)(2,1)S(1)} copy-done((bf16[1,1,96,128,128]{4,3,2,1,0:T(8,128)(2,1)S(1)}, bf16[1,1,96,128,128]{4,3,2,1,0:T(8,128)(2,1)}, u32[]{:S(2)}) %copy-start) | copy-done | bytes 3145752
  65.7 0.0 copy-start.2
  65.7 0.7 copy-done.2
  66.4 0.0 copy-start.3
  66.4 0.7 copy-done.3
  67.1 0.0 copy-start.4
  67.1 0.7 copy-done.4
  67.7 13.6 %terms.1.part_ref = bf16[128,32,128]{2,1,0:T(8,128)(2,1)S(1)} custom-call(s32[96]{0:T(128)S(1)} %bitcast.10, s32[96]{0:T(128)S(1)} %bitcast.11, s32[4,4,96]{2,1,0:T(4,128)S(1)} %bitcast.9, bf16[96,128,128]{2,1,0:T(8,128)(2,1)S(1)} %bitcast.7, bf16[32,128,256]{2,1,0:T(8,128)(2,1)S(1)} %get-tuple-element.7.row_ref, ...), custom_call_target="tpu_custom_call" | custom-call | tf_op jit(solution)/shard_map/terms/pallas_call | solution.py:318
  81.3 28.9 %sums.1 = bf16[8,4096]{1,0:T(8,128)(2,1)S(1)} custom-call(bf16[128,32,128]{2,1,0:T(8,128)(2,1)S(1)} %terms.1.part_ref), custom_call_target="tpu_custom_call" | custom-call | tf_op jit(solution)/shard_map/sums/pallas_call | solution.py:371
  110.2 0.6 copy.7
Async XLA Ops:
  0.0 0.9 copy-start.1
  63.8 1.9 %copy-start = (bf16[1,1,96,128,128]{4,3,2,1,0:T(8,128)(2,1)S(1)}, bf16[1,1,96,128,128]{4,3,2,1,0:T(8,128)(2,1)}, u32[]{:S(2)}) copy-start(bf16[1,1,96,128,128]{4,3,2,1,0:T(8,128)(2,1)} %param.5) | copy-start | bytes 9437188
  65.7 0.7 copy-start.2
  66.4 0.7 copy-start.3
  67.1 0.7 copy-start.4

commit v3 on v2

--- a/solution.py
+++ b/solution.py
@@ -327,70 +327,109 @@
     )(a_rows, a_cols, jnp.transpose(slots, (1, 2, 0)), a_blocks, row_panel, col_panel)
 
 
-def sums_kernel(ncol, part_ref, out_ref, landed, own_sem, send_sem, recv_sem):
+def sums_kernel(dims, part_ref, out_ref, landed, middle, last, send_sem, recv_sem, send_last, recv_last):
+    _, ny, nx = dims
     r, c = lax.axis_index("row"), lax.axis_index("col")
-    share = out_ref.shape[0]
+    y, x = c // nx, c % nx
+    half = out_ref.shape[0] // 2
+    steps_x = [gray(v) for v in range(1, nx)]
+    steps_y = [gray(v) for v in range(1, ny)]
+    first, second = pl.ds(0, half), pl.ds(half, half)
+
     barrier = pltpu.get_barrier_semaphore()
-    for d in range(1, ncol):
-        pl.semaphore_signal(barrier, inc=1, device_id=(r, (c + d) % ncol), device_id_type=MESH)
-    pl.semaphore_wait(barrier, ncol - 1)
-
-    def copy(d):
-        target = (c + d) % ncol
+    peers = [(r, y * nx + (x + d) % nx) for d in steps_x] + [(r, (y + d) % ny * nx + x) for d in steps_y]
+    for peer in peers:
+        pl.semaphore_signal(barrier, inc=1, device_id=peer, device_id_type=MESH)
+    pl.semaphore_wait(barrier, len(peers))
+
+    def remote(src, dst, send, recv, target):
         return pltpu.make_async_remote_copy(
-            src_ref=part_ref.at[pl.ds(target * share, share)],
-            dst_ref=landed.at[d],
-            send_sem=send_sem.at[d],
-            recv_sem=recv_sem.at[d],
-            device_id=(r, target),
-            device_id_type=MESH,
+            src_ref=src, dst_ref=dst, send_sem=send, recv_sem=recv, device_id=(r, target), device_id_type=MESH
         )
 
-    for d in range(1, ncol):
-        copy(d).start()
-    mine = pltpu.make_async_copy(part_ref.at[pl.ds(c * share, share)], landed.at[0], own_sem)
-    mine.start()
-    mine.wait()
-    for d in range(1, ncol):
-        copy(d).wait_recv()
-    for d in range(1, ncol):
-        copy(d).wait_send()
-    rows, lanes = landed.shape[2:]
-    total = landed[0].astype(F32)
-    for d in range(1, ncol):
-        total = total + landed[d].astype(F32)
+    def copy(way, d):
+        if way == 0:
+            x1 = (x + d) % nx
+            src, target = part_ref.at[:, x1, first], y * nx + x1
+        else:
+            y1 = (y + d) % ny
+            src, target = part_ref.at[y1, :, second], y1 * nx + x
+        return remote(src, landed.at[way, d], send_sem.at[way, d], recv_sem.at[way, d], target)
+
+    def copy_last(way, d):
+        i = (y + d) % ny if way == 0 else (x + d) % nx
+        target = i * nx + x if way == 0 else y * nx + i
+        return remote(middle.at[way, d], last.at[way, d], send_last.at[way, d], recv_last.at[way, d], target)
+
+    steps = (steps_x, steps_y)
+    for dx, dy in zip(*steps):
+        copy(0, dx).start()
+        copy(1, dy).start()
+    for way in (0, 1):
+        for d in steps[way]:
+            copy(way, d).wait_recv()
+
+    def summed(way, i):
+        own = part_ref[i, x, first] if way == 0 else part_ref[y, i, second]
+        total = own.astype(F32)
+        for d in steps[way]:
+            total = total + landed[way, d, i].astype(F32)
+        return total
+
+    for dy, dx in zip(steps_y, steps_x):
+        middle[0, dy] = summed(0, (y + dy) % ny)
+        copy_last(0, dy).start()
+        middle[1, dx] = summed(1, (x + dx) % nx)
+        copy_last(1, dx).start()
+    totals = [summed(0, y), summed(1, x)]
+    for way in (0, 1):
+        for d in steps[1 - way]:
+            copy_last(way, d).wait_recv()
+            totals[way] = totals[way] + last[way, d]
+    total = jnp.concatenate(totals, axis=0)
+    rows, lanes = total.shape[1:]
     for i in range(rows):
         out_ref[:, i * lanes : (i + 1) * lanes] = total[:, i, :].astype(BF16)
-
-
-def sum_at_owner(partial, ncol):
+    for way in (0, 1):
+        for d in steps[way]:
+            copy(way, d).wait_send()
+        for d in steps[1 - way]:
+            copy_last(way, d).wait_send()
+
+
+def sum_at_owner(partial, dims):
+    _, ny, nx = dims
+    assert ny == nx
     slots, rows, lanes = partial.shape
-    share = slots // ncol
+    share = slots // (ny * nx)
+    half = (share // 2, rows, lanes)
     vmem = pl.BlockSpec(memory_space=pltpu.VMEM)
     dma = pltpu.SemaphoreType.DMA
     return pl.pallas_call(
-        functools.partial(sums_kernel, ncol),
+        functools.partial(sums_kernel, dims),
         out_shape=jax.ShapeDtypeStruct((share, rows * lanes), BF16),
         in_specs=[vmem],
         out_specs=vmem,
         scratch_shapes=[
-            pltpu.VMEM((ncol, share, rows, lanes), BF16),
-            dma,
-            dma((ncol,)),
-            dma((ncol,)),
+            pltpu.VMEM((2, nx, nx, *half), BF16),
+            pltpu.VMEM((2, nx, *half), F32),
+            pltpu.VMEM((2, nx, *half), F32),
+            dma((2, nx)),
+            dma((2, nx)),
+            dma((2, nx)),
+            dma((2, nx)),
         ],
         compiler_params=pltpu.CompilerParams(collective_id=1, has_side_effects=True, vmem_limit_bytes=16 << 20),
         name="sums",
-    )(partial)
+    )(partial.reshape(ny, nx, share, rows, lanes))
 
 
 def on_device(dims, slot_count, a_blocks, a_rows, a_cols, p_blocks, coarse_slot):
-    ncol = dims[1] * dims[2]
     row_panel, col_panel = panels(p_blocks, dims)
     partial = local_terms(
         a_blocks[0, 0], a_rows[0, 0], a_cols[0, 0], coarse_slot[0, 0], row_panel, col_panel, slot_count
     )
-    return sum_at_owner(partial, ncol)[None]
+    return sum_at_owner(partial, dims)[None]
 
 
 def solution(mesh, dims=(16, 4, 4), slot_count=128):

time: 111 us -> 108 us (0.973)
  Pallas kernels: 105 us -> 101 us
    pallas_call x1, Pallas kernels: 28.9 us -> 24.9 us  [sum_at_owner(): pl.pallas_call(functools.partial(sums_kernel, dims), out_shape=jax.ShapeD...]
where the time goes in v3:
time: 108 us; the launch traced here: 107 us
  Pallas kernels  101 us (94%)
  local copies, waits for them, and re-layouts  5.43 us (5%)
    pallas_call x1, Pallas kernels, panels(): pl.pallas_call(functools.partial(panels_kernel, dims), out_shape=(jax.Sha...  62.9 us
    pallas_call x1, Pallas kernels, sum_at_owner(): pl.pallas_call(functools.partial(sums_kernel, dims), out_shape=jax.ShapeD...  24.9 us
    pallas_call x1, Pallas kernels, local_terms(): pl.pallas_call(functools.partial(terms_kernel), out_shape=jax.ShapeDtypeS...  13.6 us
    unnamed x11, local copies, waits for them, and re-layouts  5.43 us

profile of v3, /device:TPU:1, one launch (start us, length us, event | category | flops | bytes accessed | tf_op | source)
XLA Modules:
  0.0 106.8 jit_solution(13306659167644646725)
XLA Ops:
  0.0 0.0 copy-start.1
  0.0 0.9 copy-done.1
  0.9 62.9 %panels.1 = (bf16[32,128,256]{2,1,0:T(8,128)(2,1)S(1)}, bf16[64,128,256]{2,1,0:T(8,128)(2,1)S(1)}) custom-call(bf16[2,128,256]{2,1,0:T(8,128)(2,1)S(1)} %copy-done.1), custom_call_target="tpu_custom_call" | custom-call | tf_op jit(solution)/shard_map/panels/pallas_call | solution.py:231
  63.8 0.0 copy-start
  63.8 1.9 %copy-done = bf16[1,1,96,128,128]{4,3,2,1,0:T(8,128)(2,1)S(1)} copy-done((bf16[1,1,96,128,128]{4,3,2,1,0:T(8,128)(2,1)S(1)}, bf16[1,1,96,128,128]{4,3,2,1,0:T(8,128)(2,1)}, u32[]{:S(2)}) %copy-start) | copy-done | bytes 3145752
  65.7 0.0 copy-start.2
  65.7 0.7 copy-done.2
  66.4 0.0 copy-start.3
  66.4 0.7 copy-done.3
  67.1 0.0 copy-start.4
  67.1 0.7 copy-done.4
  67.7 13.6 %terms.1 = bf16[128,32,128]{2,1,0:T(8,128)(2,1)S(1)} custom-call(s32[96]{0:T(128)S(1)} %bitcast.12, s32[96]{0:T(128)S(1)} %bitcast.13, s32[4,4,96]{2,1,0:T(4,128)S(1)} %bitcast.11, bf16[96,128,128]{2,1,0:T(8,128)(2,1)S(1)} %bitcast.9, bf16[32,128,256]{2,1,0:T(8,128)(2,1)S(1)} %get-tuple-element.7.row_ref, bf16[64,128,256]{2,1,0:T(8,128)(2,1)S(1)} %get-tuple-element.8.col_ref), custom_call_target="tpu_custom_call" | custom-call | tf_op jit(solution)/shard_map/terms/pallas_call | solution.py:318
  81.3 24.9 %sums.1 = bf16[8,4096]{1,0:T(8,128)(2,1)S(1)} custom-call(bf16[4,4,8,32,128]{4,3,2,1,0:T(8,128)(2,1)S(1)} %bitcast.8), custom_call_target="tpu_custom_call" | custom-call | tf_op jit(solution)/shard_map/sums/pallas_call | solution.py:408
  106.2 0.6 copy.7
Async XLA Ops:
  0.0 0.9 copy-start.1
  63.8 1.9 %copy-start = (bf16[1,1,96,128,128]{4,3,2,1,0:T(8,128)(2,1)S(1)}, bf16[1,1,96,128,128]{4,3,2,1,0:T(8,128)(2,1)}, u32[]{:S(2)}) copy-start(bf16[1,1,96,128,128]{4,3,2,1,0:T(8,128)(2,1)} %param.5) | copy-start | bytes 9437188
  65.7 0.7 copy-start.2
  66.4 0.7 copy-start.3
  67.1 0.7 copy-start.4

commit v4 on v3

--- a/solution.py
+++ b/solution.py
@@ -234,7 +234,7 @@
             jax.ShapeDtypeStruct((2 * ncol, node, width), BF16),
             jax.ShapeDtypeStruct((4 * ncol, node, width), BF16),
         ),
-        in_specs=[vmem],
+        in_specs=[pl.BlockSpec(memory_space=pltpu.HBM)],
         out_specs=(vmem, vmem),
         scratch_shapes=[
             pltpu.VMEM((ny, nx, 2, node, width), BF16),
@@ -252,12 +252,22 @@
         ],
         compiler_params=pltpu.CompilerParams(collective_id=0, has_side_effects=True, vmem_limit_bytes=16 << 20),
         name="panels",
-    )(p_blocks)
-
-
-def terms_kernel(rows_ref, cols_ref, slots_ref, a_ref, row_ref, col_ref, out_ref, turned, left_ref, *totals):
+    )(pltpu.with_memory_space_constraint(p_blocks, pltpu.HBM))
+
+
+def terms_kernel(
+    rows_hbm, cols_hbm, slots_hbm, a_hbm, row_ref, col_ref, out_ref, sem, rows_ref, cols_ref, slots_ref, a_ref, turned, left_ref, *totals
+):
     count, width, node = left_ref.shape
     panel_rows = row_ref.shape[0]
+    fetches = [
+        pltpu.make_async_copy(src, dst, sem.at[i])
+        for i, (src, dst) in enumerate(
+            ((a_hbm, a_ref), (rows_hbm, rows_ref), (cols_hbm, cols_ref), (slots_hbm, slots_ref))
+        )
+    ]
+    for fetch in fetches:
+        fetch.start()
     agg = width // KP
     half = agg // 2
 
@@ -279,6 +289,9 @@
             turned[g * 8 + i] = lax.dot_general(
                 pick, row_ref[g * 8 + i], (((1,), (1,)), ((), ())), preferred_element_type=F32
             ).astype(BF16)
+
+    for fetch in fetches:
+        fetch.wait()
 
     @pl.loop(0, count // GROUP)
     def _(g):
@@ -314,17 +327,21 @@
     count = a_blocks.shape[0]
     panel_rows, node, width = row_panel.shape
     agg = width // KP
-    vmem, smem = pl.BlockSpec(memory_space=pltpu.VMEM), pl.BlockSpec(memory_space=pltpu.SMEM)
+    slots = jnp.transpose(slots, (1, 2, 0))
+    vmem, hbm = pl.BlockSpec(memory_space=pltpu.VMEM), pl.BlockSpec(memory_space=pltpu.HBM)
     return pl.pallas_call(
         functools.partial(terms_kernel),
         out_shape=jax.ShapeDtypeStruct((slot_count, agg // 2, 2 * agg), BF16),
-        in_specs=[smem, smem, smem, vmem, vmem, vmem],
+        in_specs=[hbm, hbm, hbm, hbm, vmem, vmem],
         out_specs=vmem,
-        scratch_shapes=[pltpu.VMEM((panel_rows, width, node), BF16), pltpu.VMEM((count, width, node), BF16)]
+        scratch_shapes=[pltpu.SemaphoreType.DMA((4,))]
+        + [pltpu.SMEM(ids.shape, jnp.int32) for ids in (a_rows, a_cols, slots)]
+        + [pltpu.VMEM(a_blocks.shape, BF16)]
+        + [pltpu.VMEM((panel_rows, width, node), BF16), pltpu.VMEM((count, width, node), BF16)]
         + [pltpu.VMEM((slot_count, agg // 2, 2 * agg), F32)] * 2,
         compiler_params=pltpu.CompilerParams(vmem_limit_bytes=36 << 20),
         name="terms",
-    )(a_rows, a_cols, jnp.transpose(slots, (1, 2, 0)), a_blocks, row_panel, col_panel)
+    )(*(pltpu.with_memory_space_constraint(v, pltpu.HBM) for v in (a_rows, a_cols, slots, a_blocks)), row_panel, col_panel)
 
 
 def sums_kernel(dims, part_ref, out_ref, landed, middle, last, send_sem, recv_sem, send_last, recv_last):

time: 108 us -> 103 us (0.954); the launches traced: 107 us -> 103 us
  local copies, waits for them, and re-layouts: 5.43 us -> 0.63 us
  Pallas kernels: 101 us -> 103 us
    unnamed x11 -> x1, local copies, waits for them, and re-layouts: 5.43 us -> 0.63 us
    pallas_call x1, Pallas kernels: 24.9 us -> 26.1 us  [sum_at_owner(): pl.pallas_call(functools.partial(sums_kernel, dims), out_shape=jax.ShapeD...]
where the time goes in v4:
time: 103 us
  Pallas kernels  103 us (100%)
    pallas_call x1, Pallas kernels, panels(): pl.pallas_call(functools.partial(panels_kernel, dims), out_shape=(jax.Sha...  63.6 us
    pallas_call x1, Pallas kernels, sum_at_owner(): pl.pallas_call(functools.partial(sums_kernel, dims), out_shape=jax.ShapeD...  26.1 us
    pallas_call x1, Pallas kernels, local_terms(): pl.pallas_call(functools.partial(terms_kernel), out_shape=jax.ShapeDtypeS...  13 us

profile of v4, /device:TPU:1, one launch (start us, length us, event | category | flops | bytes accessed | tf_op | source)
XLA Modules:
  0.0 103.2 jit_solution(11112271925588366668)
XLA Ops:
  0.0 63.6 %panels.1 = (bf16[32,128,256]{2,1,0:T(8,128)(2,1)S(1)}, bf16[64,128,256]{2,1,0:T(8,128)(2,1)S(1)}) custom-call(bf16[2,128,256]{2,1,0:T(8,128)(2,1)} %p_ref.1), custom_call_target="tpu_custom_call" | custom-call | tf_op jit(solution)/shard_map/panels/pallas_call | solution.py:231
  63.6 13.0 %terms.1 = bf16[128,32,128]{2,1,0:T(8,128)(2,1)S(1)} custom-call(s32[96]{0:T(128)} %bitcast.12, s32[96]{0:T(128)} %bitcast.13, s32[4,4,96]{2,1,0:T(4,128)} %bitcast.11, bf16[96,128,128]{2,1,0:T(8,128)(2,1)} %bitcast.10, bf16[32,128,256]{2,1,0:T(8,128)(2,1)S(1)} %get-tuple-element.7.row_ref, bf16[64,128,256]{2,1,0:T(8,128)(2,1)S(1)} %get-tuple-element.8.col_ref), custom_call_target="tpu_custom_call" | custom-call | tf_op jit(solution)/shard_map/terms/pallas_call | solution.py:332
  76.6 26.1 %sums.1 = bf16[8,4096]{1,0:T(8,128)(2,1)S(1)} custom-call(bf16[4,4,8,32,128]{4,3,2,1,0:T(8,128)(2,1)S(1)} %bitcast.8), custom_call_target="tpu_custom_call" | custom-call | tf_op jit(solution)/shard_map/sums/pallas_call | solution.py:425
  102.6 0.6 copy.7

commit v5 on v3

--- a/solution.py
+++ b/solution.py
@@ -12,7 +12,7 @@
 
 HOP = 4
 KP = 4
-GROUP = 16
+GROUP = 24
 PARTS = 2
 
 
@@ -20,7 +20,8 @@
     return v + v // 2 - 2 * ((v // 2) * (v % 2))
 
 
-def panels_kernel(dims, p_ref, row_ref, col_ref, passing, own_sem, g_send, g_recv, r_send, r_recv, z_send, z_recv, a_send, a_recv, s_send, s_recv):
+def panels_kernel(
+    dims, rows_hbm, a_hbm, p_ref, left_ref, col_ref, rows_ref, a_ref, row_ref, turned, passing, own_sem, g_send, g_recv, r_send, r_recv, z_send, z_recv, a_send, a_recv, s_send, s_recv):
     nz, ny, nx = dims
     ncol = ny * nx
     r, c = lax.axis_index("row"), lax.axis_index("col")
@@ -107,6 +108,12 @@
             z_copy(1, plane, x, j).start()
         deliver(plane, x)
 
+    fetches = [
+        pltpu.make_async_copy(rows_hbm, rows_ref, own_sem.at[2]),
+        pltpu.make_async_copy(a_hbm, a_ref, own_sem.at[3]),
+    ]
+    for fetch in fetches:
+        fetch.start()
     mine = pltpu.make_async_copy(p_ref, row_ref.at[pl.ds(2 * c, 2)], own_sem.at[0])
     mine.start()
     for d in steps_y:
@@ -171,6 +178,34 @@
                 def _():
                     relay(way, feed, n)
 
+    for u in range(ny):
+        for v in range(1, nx):
+            arrived(((y + u) % ny) * nx + (x + v) % nx)
+    mine.wait()
+    for fetch in fetches:
+        fetch.wait()
+    count, node, _ = a_ref.shape
+    panel_rows, _, width = row_ref.shape
+    agg = width // KP
+    to = lax.broadcasted_iota(jnp.int32, (width, width), 0)
+    at = lax.broadcasted_iota(jnp.int32, (width, width), 1)
+    inner = to % agg
+    source = to - inner + 2 * (inner % (agg // 2)) + inner // (agg // 2)
+    pick = jnp.where(at == source, 1.0, 0.0).astype(BF16)
+
+    @pl.loop(0, panel_rows // 8)
+    def _(g):
+        for i in range(8):
+            turned[g * 8 + i] = lax.dot_general(
+                pick, row_ref[g * 8 + i], (((1,), (1,)), ((), ())), preferred_element_type=F32
+            ).astype(BF16)
+
+    @pl.loop(0, count // GROUP)
+    def _(g):
+        for i in range(GROUP):
+            k = g * GROUP + i
+            left_ref[k] = jnp.dot(turned[rows_ref[k]], a_ref[k], preferred_element_type=F32).astype(BF16)
+
     def s_copy(c0):
         rows = col_ref.at[pl.ds(base + 2 * c0, 2)]
         return remote(rows, rows, s_send.at[c0], s_recv.at[c0], (sibling, c))
@@ -182,10 +217,6 @@
         remote(passing.at[0, 0], rows, a_send.at[0, 0], a_recv.at[c0], (r, c)).wait_recv()
         s_copy(c0).start()
 
-    for u in range(ny):
-        for v in range(1, nx):
-            arrived(((y + u) % ny) * nx + (x + v) % nx)
-    mine.wait()
     for copy in sends:
         copy.wait_send()
 
@@ -222,23 +253,28 @@
         s_copy(c0).wait_recv()
 
 
-def panels(p_blocks, dims):
+def panels(a_blocks, a_rows, p_blocks, dims):
     nz, ny, nx = dims
     ncol = ny * nx
+    count = a_blocks.shape[0]
     _, node, width = p_blocks.shape
     vmem = pl.BlockSpec(memory_space=pltpu.VMEM)
     dma = pltpu.SemaphoreType.DMA
     return pl.pallas_call(
         functools.partial(panels_kernel, dims),
         out_shape=(
-            jax.ShapeDtypeStruct((2 * ncol, node, width), BF16),
+            jax.ShapeDtypeStruct((count, width, node), BF16),
             jax.ShapeDtypeStruct((4 * ncol, node, width), BF16),
         ),
-        in_specs=[vmem],
+        in_specs=[pl.BlockSpec(memory_space=pltpu.HBM)] * 3,
         out_specs=(vmem, vmem),
         scratch_shapes=[
+            pltpu.SMEM(a_rows.shape, jnp.int32),
+            pltpu.VMEM(a_blocks.shape, BF16),
+            pltpu.VMEM((2 * ncol, node, width), BF16),
+            pltpu.VMEM((2 * ncol, width, node), BF16),
             pltpu.VMEM((ny, nx, 2, node, width), BF16),
-            dma((2,)),
+            dma((4,)),
             dma,
             dma((nx,)),
             dma((ncol - 1,)),
@@ -250,16 +286,21 @@
             dma((ncol,)),
             dma((ncol,)),
         ],
-        compiler_params=pltpu.CompilerParams(collective_id=0, has_side_effects=True, vmem_limit_bytes=16 << 20),
+        compiler_params=pltpu.CompilerParams(collective_id=0, has_side_effects=True, vmem_limit_bytes=24 << 20),
         name="panels",
-    )(p_blocks)
-
-
-def terms_kernel(rows_ref, cols_ref, slots_ref, a_ref, row_ref, col_ref, out_ref, turned, left_ref, *totals):
-    count, width, node = left_ref.shape
-    panel_rows = row_ref.shape[0]
+    )(*(pltpu.with_memory_space_constraint(v, pltpu.HBM) for v in (a_rows, a_blocks, p_blocks)))
+
+
+def terms_kernel(cols_hbm, slots_hbm, left_ref, col_ref, out_ref, sem, cols_ref, slots_ref, *totals):
+    count, width, _ = left_ref.shape
     agg = width // KP
     half = agg // 2
+    fetches = [
+        pltpu.make_async_copy(cols_hbm, cols_ref, sem.at[0]),
+        pltpu.make_async_copy(slots_hbm, slots_ref, sem.at[1]),
+    ]
+    for fetch in fetches:
+        fetch.start()
 
     @pl.loop(0, out_ref.shape[0] // 8)
     def _(g):
@@ -267,24 +308,8 @@
         for total in totals:
             total[some] = jnp.zeros((8, *total.shape[1:]), F32)
 
-    to = lax.broadcasted_iota(jnp.int32, (width, width), 0)
-    at = lax.broadcasted_iota(jnp.int32, (width, width), 1)
-    inner = to % agg
-    source = to - inner + 2 * (inner % half) + inner // half
-    pick = jnp.where(at == source, 1.0, 0.0).astype(BF16)
-
-    @pl.loop(0, panel_rows // 8)
-    def _(g):
-        for i in range(8):
-            turned[g * 8 + i] = lax.dot_general(
-                pick, row_ref[g * 8 + i], (((1,), (1,)), ((), ())), preferred_element_type=F32
-            ).astype(BF16)
-
-    @pl.loop(0, count // GROUP)
-    def _(g):
-        for i in range(GROUP):
-            k = g * GROUP + i
-            left_ref[k] = jnp.dot(turned[rows_ref[k]], a_ref[k], preferred_element_type=F32).astype(BF16)
+    for fetch in fetches:
+        fetch.wait()
 
     low = lax.broadcasted_iota(jnp.int32, (half, 2 * agg), 1) < agg
 
@@ -310,21 +335,21 @@
         out_ref[some] = functools.reduce(lambda p, q: p + q, [total[some] for total in totals]).astype(BF16)
 
 
-def local_terms(a_blocks, a_rows, a_cols, slots, row_panel, col_panel, slot_count):
-    count = a_blocks.shape[0]
-    panel_rows, node, width = row_panel.shape
-    agg = width // KP
-    vmem, smem = pl.BlockSpec(memory_space=pltpu.VMEM), pl.BlockSpec(memory_space=pltpu.SMEM)
+def local_terms(left, a_cols, slots, col_panel, slot_count):
+    agg = left.shape[1] // KP
+    slots = jnp.transpose(slots, (1, 2, 0))
+    vmem, hbm = pl.BlockSpec(memory_space=pltpu.VMEM), pl.BlockSpec(memory_space=pltpu.HBM)
     return pl.pallas_call(
         functools.partial(terms_kernel),
         out_shape=jax.ShapeDtypeStruct((slot_count, agg // 2, 2 * agg), BF16),
-        in_specs=[smem, smem, smem, vmem, vmem, vmem],
+        in_specs=[hbm, hbm, vmem, vmem],
         out_specs=vmem,
-        scratch_shapes=[pltpu.VMEM((panel_rows, width, node), BF16), pltpu.VMEM((count, width, node), BF16)]
+        scratch_shapes=[pltpu.SemaphoreType.DMA((2,))]
+        + [pltpu.SMEM(ids.shape, jnp.int32) for ids in (a_cols, slots)]
         + [pltpu.VMEM((slot_count, agg // 2, 2 * agg), F32)] * 2,
-        compiler_params=pltpu.CompilerParams(vmem_limit_bytes=36 << 20),
+        compiler_params=pltpu.CompilerParams(vmem_limit_bytes=24 << 20),
         name="terms",
-    )(a_rows, a_cols, jnp.transpose(slots, (1, 2, 0)), a_blocks, row_panel, col_panel)
+    )(*(pltpu.with_memory_space_constraint(v, pltpu.HBM) for v in (a_cols, slots)), left, col_panel)
 
 
 def sums_kernel(dims, part_ref, out_ref, landed, middle, last, send_sem, recv_sem, send_last, recv_last):
@@ -425,10 +450,8 @@
 
 
 def on_device(dims, slot_count, a_blocks, a_rows, a_cols, p_blocks, coarse_slot):
-    row_panel, col_panel = panels(p_blocks, dims)
-    partial = local_terms(
-        a_blocks[0, 0], a_rows[0, 0], a_cols[0, 0], coarse_slot[0, 0], row_panel, col_panel, slot_count
-    )
+    left, col_panel = panels(a_blocks[0, 0], a_rows[0, 0], p_blocks, dims)
+    partial = local_terms(left, a_cols[0, 0], coarse_slot[0, 0], col_panel, slot_count)
     return sum_at_owner(partial, dims)[None]
 
 

time: 108 us -> 99.2 us (0.919)
  local copies, waits for them, and re-layouts: 5.43 us -> 0.63 us
  Pallas kernels: 101 us -> 98.3 us
    pallas_call x1, Pallas kernels: 13.6 us -> 8.59 us  [local_terms(): pl.pallas_call(functools.partial(terms_kernel), out_shape=jax.ShapeDtypeS...]
    unnamed x11 -> x1, local copies, waits for them, and re-layouts: 5.43 us -> 0.63 us
    pallas_call x1, Pallas kernels: 62.9 us -> 67.7 us  [panels(): pl.pallas_call(functools.partial(panels_kernel, dims), out_shape=(jax.Sha...]
    pallas_call x1, Pallas kernels: 24.9 us -> 22 us  [sum_at_owner(): pl.pallas_call(functools.partial(sums_kernel, dims), out_shape=jax.ShapeD...]
where the time goes in v5:
time: 99.2 us; the launch traced here: 99 us
  Pallas kernels  98.3 us (99%)
    pallas_call x1, Pallas kernels, panels(): pl.pallas_call(functools.partial(panels_kernel, dims), out_shape=(jax.Sha...  67.7 us
    pallas_call x1, Pallas kernels, sum_at_owner(): pl.pallas_call(functools.partial(sums_kernel, dims), out_shape=jax.ShapeD...  22 us
    pallas_call x1, Pallas kernels, local_terms(): pl.pallas_call(functools.partial(terms_kernel), out_shape=jax.ShapeDtypeS...  8.59 us

profile of v5, /device:TPU:1, one launch (start us, length us, event | category | flops | bytes accessed | tf_op | source)
XLA Modules:
  0.0 99.0 jit_solution(2975944774730517589)
XLA Ops:
  0.0 67.7 %panels.1 = (bf16[96,256,128]{2,1,0:T(8,128)(2,1)S(1)}, bf16[64,128,256]{2,1,0:T(8,128)(2,1)S(1)}) custom-call(s32[96]{0:T(128)} %bitcast.13, bf16[96,128,128]{2,1,0:T(8,128)(2,1)} %bitcast.10, bf16[2,128,256]{2,1,0:T(8,128)(2,1)} %p_ref.1), custom_call_target="tpu_custom_call" | custom-call | tf_op jit(solution)/shard_map/panels/pallas_call | solution.py:263
  67.7 8.6 %terms.1 = bf16[128,32,128]{2,1,0:T(8,128)(2,1)S(1)} custom-call(s32[96]{0:T(128)} %bitcast.12, s32[4,4,96]{2,1,0:T(4,128)} %bitcast.11, bf16[96,256,128]{2,1,0:T(8,128)(2,1)S(1)} %get-tuple-element.7.left_ref, bf16[64,128,256]{2,1,0:T(8,128)(2,1)S(1)} %get-tuple-element.8.col_ref), custom_call_target="tpu_custom_call" | custom-call | tf_op jit(solution)/shard_map/terms/pallas_call | solution.py:342
  76.3 22.0 %sums.1 = bf16[8,4096]{1,0:T(8,128)(2,1)S(1)} custom-call(bf16[4,4,8,32,128]{4,3,2,1,0:T(8,128)(2,1)S(1)} %bitcast.8), custom_call_target="tpu_custom_call" | custom-call | tf_op jit(solution)/shard_map/sums/pallas_call | solution.py:433
  98.3 0.6 copy.7

commit v6 on v5

--- a/solution.py
+++ b/solution.py
@@ -68,19 +68,21 @@
         o = pos if way == 0 else (nx - pos) % nx
         return (x + o) % nx, (o < nx // 2 if way == 0 else o >= nx // 2)
 
-    def a_copy(y1, x0):
-        rows = col_ref.at[pl.ds(base + 2 * (y * nx + x0), 2)]
-        return remote(passing.at[y1, x0], rows, a_send.at[y1, x0], a_recv.at[y * nx + x0], (r, y1 * nx + x))
-
-    def deliver(y1, x0):
+    def a_copy(y1, x0, row):
+        piece = y * nx + x0
+        dst = col_ref.at[base + 2 * piece + row]
+        return remote(passing.at[y1, x0, row], dst, a_send.at[y1, x0, row], a_recv.at[piece, row], (r, y1 * nx + x))
+
+    def deliver(y1, x0, row):
         @pl.when(y1 != y)
         def _():
-            a_copy(y1, x0).start()
+            a_copy(y1, x0, row).start()
 
         @pl.when(y1 == y)
         def _():
-            rows = col_ref.at[pl.ds(base + 2 * (y * nx + x0), 2)]
-            pltpu.make_async_copy(passing.at[y1, x0], rows, a_recv.at[y * nx + x0]).start()
+            piece = y * nx + x0
+            dst = col_ref.at[base + 2 * piece + row]
+            pltpu.make_async_copy(passing.at[y1, x0, row], dst, a_recv.at[piece, row]).start()
 
     sends = []
 
@@ -106,7 +108,8 @@
         for j in range(2 * PARTS):
             z_copy(0, plane, x, j).start()
             z_copy(1, plane, x, j).start()
-        deliver(plane, x)
+        deliver(plane, x, 0)
+        deliver(plane, x, 1)
 
     fetches = [
         pltpu.make_async_copy(rows_hbm, rows_ref, own_sem.at[2]),
@@ -132,7 +135,8 @@
             for j in range(2 * PARTS):
                 z_copy(0, plane, a, j).start()
                 z_copy(1, plane, b, j).start()
-            deliver(plane, a)
+            deliver(plane, a, 0)
+            deliver(plane, a, 1)
 
     for d in steps_y:
         piece = along_y(d)
@@ -164,9 +168,9 @@
             def _():
                 z_copy(way, y1, x0, j).start()
 
-            @pl.when(j == parts - 1)
+            @pl.when(j % PARTS == PARTS - 1)
             def _():
-                deliver(y1, x0)
+                deliver(y1, x0, j // PARTS)
 
     @pl.loop(0, chunks + HOP * (far - 1))
     def _(step):
@@ -213,8 +217,9 @@
     @pl.loop(0, ncol)
     def _(i):
         c0 = (c + i) % ncol
-        rows = col_ref.at[pl.ds(base + 2 * c0, 2)]
-        remote(passing.at[0, 0], rows, a_send.at[0, 0], a_recv.at[c0], (r, c)).wait_recv()
+        for row in (0, 1):
+            here = col_ref.at[base + 2 * c0 + row]
+            remote(here, here, a_send.at[0, 0, 0], a_recv.at[c0, row], (r, c)).wait_recv()
         s_copy(c0).start()
 
     for copy in sends:
@@ -235,7 +240,8 @@
         for y1 in range(ny):
             @pl.when(y1 != y)
             def _():
-                a_copy(y1, x0).wait_send()
+                a_copy(y1, x0, 0).wait_send()
+                a_copy(y1, x0, 1).wait_send()
 
     @pl.loop(0, chunks)
     def _(n):
@@ -281,8 +287,8 @@
             dma((ncol,)),
             dma((2, ny, nx, 2 * PARTS)),
             dma((2, ny, nx, 2 * PARTS)),
-            dma((ny, nx)),
-            dma((ncol,)),
+            dma((ny, nx, 2)),
+            dma((ncol, 2)),
             dma((ncol,)),
             dma((ncol,)),
         ],
@@ -372,14 +378,14 @@
             src_ref=src, dst_ref=dst, send_sem=send, recv_sem=recv, device_id=(r, target), device_id_type=MESH
         )
 
-    def copy(way, d):
+    def copy(way, d, e):
         if way == 0:
-            x1 = (x + d) % nx
-            src, target = part_ref.at[:, x1, first], y * nx + x1
+            i, x1 = (y + e) % ny, (x + d) % nx
+            src, target = part_ref.at[i, x1, first], y * nx + x1
         else:
-            y1 = (y + d) % ny
-            src, target = part_ref.at[y1, :, second], y1 * nx + x
-        return remote(src, landed.at[way, d], send_sem.at[way, d], recv_sem.at[way, d], target)
+            i, y1 = (x + e) % nx, (y + d) % ny
+            src, target = part_ref.at[y1, i, second], y1 * nx + x
+        return remote(src, landed.at[way, d, i], send_sem.at[way, d, e], recv_sem.at[way, d, e], target)
 
     def copy_last(way, d):
         i = (y + d) % ny if way == 0 else (x + d) % nx
@@ -387,14 +393,15 @@
         return remote(middle.at[way, d], last.at[way, d], send_last.at[way, d], recv_last.at[way, d], target)
 
     steps = (steps_x, steps_y)
-    for dx, dy in zip(*steps):
-        copy(0, dx).start()
-        copy(1, dy).start()
-    for way in (0, 1):
+    for e in (*steps_y, 0):
+        for dx, dy in zip(*steps):
+            copy(0, dx, e).start()
+            copy(1, dy, e).start()
+
+    def summed(way, e):
         for d in steps[way]:
-            copy(way, d).wait_recv()
-
-    def summed(way, i):
+            copy(way, d, e).wait_recv()
+        i = (y + e) % ny if way == 0 else (x + e) % nx
         own = part_ref[i, x, first] if way == 0 else part_ref[y, i, second]
         total = own.astype(F32)
         for d in steps[way]:
@@ -402,11 +409,11 @@
         return total
 
     for dy, dx in zip(steps_y, steps_x):
-        middle[0, dy] = summed(0, (y + dy) % ny)
+        middle[0, dy] = summed(0, dy)
         copy_last(0, dy).start()
-        middle[1, dx] = summed(1, (x + dx) % nx)
+        middle[1, dx] = summed(1, dx)
         copy_last(1, dx).start()
-    totals = [summed(0, y), summed(1, x)]
+    totals = [summed(0, 0), summed(1, 0)]
     for way in (0, 1):
         for d in steps[1 - way]:
             copy_last(way, d).wait_recv()
@@ -417,7 +424,8 @@
         out_ref[:, i * lanes : (i + 1) * lanes] = total[:, i, :].astype(BF16)
     for way in (0, 1):
         for d in steps[way]:
-            copy(way, d).wait_send()
+            for e in range(nx):
+                copy(way, d, e).wait_send()
         for d in steps[1 - way]:
             copy_last(way, d).wait_send()
 
@@ -439,8 +447,8 @@
             pltpu.VMEM((2, nx, nx, *half), BF16),
             pltpu.VMEM((2, nx, *half), F32),
             pltpu.VMEM((2, nx, *half), F32),
-            dma((2, nx)),
-            dma((2, nx)),
+            dma((2, nx, nx)),
+            dma((2, nx, nx)),
             dma((2, nx)),
             dma((2, nx)),
         ],

time: 99.2 us -> 96.4 us (0.972)
  Pallas kernels: 98.3 us -> 95.5 us
    pallas_call x1, Pallas kernels: 22 us -> 19 us  [sum_at_owner(): pl.pallas_call(functools.partial(sums_kernel, dims), out_shape=jax.ShapeD...]
where the time goes in v6:
time: 96.4 us; the launch traced here: 96.2 us
  Pallas kernels  95.5 us (99%)
    pallas_call x1, Pallas kernels, panels(): pl.pallas_call(functools.partial(panels_kernel, dims), out_shape=(jax.Sha...  68 us
    pallas_call x1, Pallas kernels, sum_at_owner(): pl.pallas_call(functools.partial(sums_kernel, dims), out_shape=jax.ShapeD...  19 us
    pallas_call x1, Pallas kernels, local_terms(): pl.pallas_call(functools.partial(terms_kernel), out_shape=jax.ShapeDtypeS...  8.59 us

profile of v6, /device:TPU:1, one launch (start us, length us, event | category | flops | bytes accessed | tf_op | source)
XLA Modules:
  0.0 96.2 jit_solution(17825920049553526098)
XLA Ops:
  0.0 68.0 %panels.1 = (bf16[96,256,128]{2,1,0:T(8,128)(2,1)S(1)}, bf16[64,128,256]{2,1,0:T(8,128)(2,1)S(1)}) custom-call(s32[96]{0:T(128)} %bitcast.13, bf16[96,128,128]{2,1,0:T(8,128)(2,1)} %bitcast.10, bf16[2,128,256]{2,1,0:T(8,128)(2,1)} %p_ref.1), custom_call_target="tpu_custom_call" | custom-call | tf_op jit(solution)/shard_map/panels/pallas_call | solution.py:269
  68.0 8.6 %terms.1 = bf16[128,32,128]{2,1,0:T(8,128)(2,1)S(1)} custom-call(s32[96]{0:T(128)} %bitcast.12, s32[4,4,96]{2,1,0:T(4,128)} %bitcast.11, bf16[96,256,128]{2,1,0:T(8,128)(2,1)S(1)} %get-tuple-element.7.left_ref, bf16[64,128,256]{2,1,0:T(8,128)(2,1)S(1)} %get-tuple-element.8.col_ref), custom_call_target="tpu_custom_call" | custom-call | tf_op jit(solution)/shard_map/terms/pallas_call | solution.py:348
  76.6 19.0 %sums.1 = bf16[8,4096]{1,0:T(8,128)(2,1)S(1)} custom-call(bf16[4,4,8,32,128]{4,3,2,1,0:T(8,128)(2,1)S(1)} %bitcast.8), custom_call_target="tpu_custom_call" | custom-call | tf_op jit(solution)/shard_map/sums/pallas_call | solution.py:441
  95.6 0.6 copy.7
